TPU v7x, 32 devices: a whole 2x2x4 slice. The times are simulated.
32 devices in a mesh: dp: 4 (over x, core), vocab: 4 (over z), tensor: 2 (over y).
Axes of the slice: x: 2, y: 2, z: 4, core: 2. Of those that a mesh axis runs over, the one named last changes fastest.
Arguments:
- residual: bfloat16 [352, 4096], P('dp', 'tensor'), may hold values from -400 to 400
- norm_gain: float32 [4096], P('tensor'), may hold values from 0.1 to 1.9
- gain_dir: float32 [4096], P('tensor'), may hold values from -6 to 6
- head_weight: bfloat16 [4096, 10240], P('tensor', ('dp', 'vocab')), may hold values from -0.8 to 0.8
- head_dir: bfloat16 [4096, 10240], P('tensor', ('dp', 'vocab')), may hold values from -0.25 to 0.25
- sampled: int32 [352], replicated, may hold values from 0 to 10239
Outputs:
- fisher_head: float32 [4096, 10240], P('tensor', ('dp', 'vocab'))
- fisher_gain: float32 [4096], P('tensor')
All inputs are finite; a program needn't handle non-finite values.
Results may differ from a plain program's by a relative error of at most 0.012.
The roundings to bfloat16 on the way count: a program that leaves them out, or rounds other values in their place, can miss the bound.
Values may be sent and summed in bfloat16 or wider, within the bound.
A program may use at most 128 MiB of HBM per device.

v0:
```python
import jax
import jax.numpy as jnp
from jax import lax
from jax.sharding import PartitionSpec as P

EPSILON = 1e-06


def local(residual, norm_gain, gain_dir, head_weight, head_dir, sampled):
    full_width = residual.shape[1] * lax.axis_size("tensor")
    entries = residual.astype(jnp.float32)
    squares = lax.psum(jnp.sum(entries * entries, axis=1), "tensor")
    normed = (entries * lax.rsqrt(squares / full_width + EPSILON)[:, None]).astype(jnp.bfloat16)
    gathered = lax.all_gather(normed, "dp", axis=0, tiled=True)
    spread = gathered.astype(jnp.float32)
    hidden = (spread * norm_gain).astype(jnp.bfloat16)
    tangent = (spread * gain_dir).astype(jnp.bfloat16)
    logits = jnp.dot(hidden, head_weight, preferred_element_type=jnp.float32)
    tangent_logits = jnp.dot(hidden, head_dir, preferred_element_type=jnp.float32) + jnp.dot(
        tangent, head_weight, preferred_element_type=jnp.float32
    )
    logits, tangent_logits = (
        lax.psum_scatter(logits, "tensor", scatter_dimension=0, tiled=True),
        lax.psum_scatter(tangent_logits, "tensor", scatter_dimension=0, tiled=True),
    )
    share_rows = logits.shape[0]
    picked_ids = lax.dynamic_slice_in_dim(
        sampled, lax.axis_index("tensor") * share_rows, share_rows
    )
    vocab_dev = head_weight.shape[1]
    offset = (lax.axis_index("dp") * lax.axis_size("vocab") + lax.axis_index("vocab")) * vocab_dev
    is_picked = lax.broadcasted_iota(jnp.int32, logits.shape, 1) == (picked_ids - offset)[:, None]
    picked_part = jnp.sum(jnp.where(is_picked, tangent_logits, 0.0), axis=1)
    row_top = lax.pmax(jnp.max(logits, axis=1), ("dp", "vocab"))
    scaled_exp = jnp.exp(logits - row_top[:, None])
    row_total, weighted, picked = lax.psum(
        (jnp.sum(scaled_exp, axis=1), jnp.sum(scaled_exp * tangent_logits, axis=1), picked_part),
        ("dp", "vocab"),
    )
    row_probs = scaled_exp / row_total[:, None]
    row_score = picked - weighted / row_total
    cotangent = (row_score[:, None] * (is_picked.astype(jnp.float32) - row_probs)).astype(
        jnp.bfloat16
    )
    full_cot = lax.all_gather(cotangent, "tensor", axis=0, tiled=True)
    product = lax.dot_general(
        gathered, full_cot, (((0,), (0,)), ((), ())), preferred_element_type=jnp.float32
    )
    fisher_head = norm_gain[:, None] * product
    fisher_gain = lax.psum(
        jnp.sum(head_weight.astype(jnp.float32) * product, axis=1), ("dp", "vocab")
    )
    return (fisher_head, fisher_gain)


def solution(mesh):
    in_specs = (
        P("dp", "tensor"),
        P("tensor"),
        P("tensor"),
        P("tensor", ("dp", "vocab")),
        P("tensor", ("dp", "vocab")),
        P(),
    )
    out_specs = (P("tensor", ("dp", "vocab")), P("tensor"))
    return jax.shard_map(local, mesh=mesh, in_specs=in_specs, out_specs=out_specs, check_vma=False)
```

profile of v0, /device:TPU:0, one launch (start us, length us, event | category | flops | bytes accessed | tf_op | source)
XLA Modules:
  0.0 185.8 jit_solution(10829255052251060643)
XLA Ops:
  7.2 0.0 copy-start
  7.2 0.0 all-gather.2.cloned.1.call-start
  7.2 1.3 fusion.12
  8.5 5.9 %psum.35 = f32[88]{0:T(128)S(1)} all-reduce(f32[88]{0:T(128)S(1)} %fusion.12), channel_id=1, replica_groups=mesh['dp'=4,'vocab'=4,'tensor'=2] {'tensor'}, use_global_device_ids=true, to_apply=%region_1.0 | all-reduce | flops 88 | bytes 704 | tf_op jit(solution)/shard_map/psum | solution.py:12
  14.4 1.9 fusion.13
  16.3 0.0 all-gather.2.cloned.1.call-update
  16.3 0.0 copy-start.3
  16.3 0.0 reduce-scatter.5.cloned.1.call-start
  16.4 20.8 %all-gather.2.cloned.1.call-done = bf16[352,2048]{1,0:T(8,128)(2,1)} async-done(((bf16[88,2048]{1,0:T(8,128)(2,1)}), bf16[352,2048]{1,0:T(8,128)(2,1)}) %all-gather.2.cloned.1.call-update) | async-done | bytes 1441808 | tf_op jit(solution)/shard_map/all_gather | solution.py:14
  37.1 4.4 %fusion.8 = f32[352,640]{1,0:T(8,128)} fusion(bf16[2048,640]{1,0:T(8,128)(2,1)} %param.9, bf16[352,2048]{1,0:T(8,128)(2,1)} %all-gather.2.cloned.1.call-done, f32[2048]{0:T(1024)} %param.7), kind=kOutput, calls=%fused_computation.9 | convolution fusion | flops 924909568 | bytes 4972544 | tf_op jit(solution)/shard_map/dot_general | solution.py:18
  41.6 0.0 reduce-scatter.5.cloned.1.call-update
  41.6 0.0 copy-start.5
  41.6 0.0 reduce-scatter.3.cloned.1.call-start
  41.6 0.0 copy-done
  41.7 0.0 copy-done.3
  41.7 0.0 copy-start.1
  41.7 0.0 copy-start.2
  41.7 2.8 %fusion.10 = f32[352,640]{1,0:T(8,128)S(1)} fusion(bf16[2048,640]{1,0:T(8,128)(2,1)S(1)} %copy-done, bf16[352,2048]{1,0:T(8,128)(2,1)} %all-gather.2.cloned.1.call-done, f32[2048]{0:T(1024)S(1)} %copy-done.3), kind=kOutput, calls=%fused_computation.10 | convolution fusion | flops 924909568 | bytes 4972544 | tf_op jit(solution)/shard_map/dot_general | solution.py:19
  44.5 0.0 copy-done.5
  44.5 0.0 copy-done.1
  44.5 0.0 copy-done.2
  44.5 2.3 %fusion.5 = f32[352,640]{1,0:T(8,128)} fusion(f32[352,640]{1,0:T(8,128)S(1)} %fusion.10, bf16[2048,640]{1,0:T(8,128)(2,1)S(1)} %copy-done.2, bf16[352,2048]{1,0:T(8,128)(2,1)S(1)} %copy-done.1, f32[2048]{0:T(1024)S(1)} %copy-done.5), kind=kOutput, calls=%fused_computation.8 | convolution fusion | flops 925134848 | bytes 5873664 | tf_op jit(solution)/shard_map/dot_general | solution.py:19
  46.8 0.0 reduce-scatter.3.cloned.1.call-update
  46.8 0.0 copy-start.4
  46.8 4.5 %copy.8 = bf16[2048,640]{0,1:T(8,128)(2,1)} copy(bf16[2048,640]{1,0:T(8,128)(2,1)} %param.9) | data formatting | bytes 5242880 | tf_op args[3]
  51.3 0.0 copy-done.4
  51.3 0.1 dynamic-slice_subtract_fusion
  51.4 9.1 %reduce-scatter.5.cloned.1.call-done = f32[176,640]{1,0:T(8,128)} async-done(((f32[352,640]{1,0:T(8,128)}), f32[176,640]{1,0:T(8,128)}) %reduce-scatter.5.cloned.1.call-update) | async-done | bytes 450576 | tf_op jit(solution)/shard_map/reduce_scatter | solution.py:23
  60.4 1.1 reduce_max.9
  61.6 33.4 %pmax.7 = f32[176]{0:T(256)S(1)} all-reduce(f32[176]{0:T(256)S(1)} %reduce_max.9), channel_id=1, replica_groups=mesh['dp'=4,'vocab'=4,'tensor'=2] {'dp','vocab'}, use_global_device_ids=true, to_apply=%region_7.8 | all-reduce | flops 176 | bytes 1408 | tf_op jit(solution)/shard_map/pmax | solution.py:34
  95.0 0.0 reduce-scatter.3.cloned.1.call-done
  95.0 1.5 multiply_reduce_fusion.1
  96.4 29.7 %all-reduce = (f32[176]{0:T(256)S(1)}, f32[176]{0:T(256)S(1)}, f32[176]{0:T(256)S(1)}) all-reduce(f32[176]{0:T(256)S(1)} %get-tuple-element.5, f32[176]{0:T(256)S(1)} %get-tuple-element.6, f32[176]{0:T(256)S(1)} %get-tuple-element.4), channel_id=1, replica_groups=mesh['dp'=4,'vocab'=4,'tensor'=2] {'dp','vocab'}, use_global_device_ids=true, to_apply=%region_11.12 | all-reduce | flops 528 | bytes 4224 | tf_op jit(solution)/shard_map/psum | solution.py:36
  126.1 1.2 multiply_convert_fusion
  127.4 6.7 %all_gather.7 = bf16[352,640]{1,0:T(8,128)(2,1)S(1)} all-gather(bf16[176,640]{1,0:T(8,128)(2,1)S(1)} %multiply_convert_fusion), channel_id=1, replica_groups=mesh['dp'=4,'vocab'=4,'tensor'=2] {'tensor'}, dimensions={0}, use_global_device_ids=true | all-gather | bytes 675840 | tf_op jit(solution)/shard_map/all_gather | solution.py:45
  134.0 6.3 %multiply_reduce_fusion = (f32[2048]{0:T(1024)S(1)}, f32[2048,640]{0,1:T(8,128)}) fusion(bf16[2048,640]{0,1:T(8,128)(2,1)} %copy.8, f32[2048]{0:T(1024)S(1)} %copy-done.3, bf16[352,2048]{1,0:T(8,128)(2,1)} %all-gather.2.cloned.1.call-done, bf16[352,640]{1,0:T(8,128)(2,1)S(1)} %all_gather.7), kind=kOutput, calls=%fused_computation | convolution fusion | flops 927987712 | bytes 9773056 | tf_op jit(solution)/shard_map/dot_general | solution.py:46
  140.3 33.1 %psum.39 = f32[2048]{0:T(1024)} all-reduce(f32[2048]{0:T(1024)S(1)} %get-tuple-element.10), channel_id=1, replica_groups=mesh['dp'=4,'vocab'=4,'tensor'=2] {'dp','vocab'}, use_global_device_ids=true, to_apply=%region_13.14 | all-reduce | flops 2048 | bytes 16384 | tf_op jit(solution)/shard_map/psum | solution.py:50
  173.4 5.9 %copy.9 = f32[2048,640]{1,0:T(8,128)} copy(f32[2048,640]{0,1:T(8,128)} %get-tuple-element.11) | data formatting | bytes 10485760
  (2 shorter events, 0.0 us)
Async XLA Ops:
  7.2 34.5 %copy-start = (bf16[2048,640]{1,0:T(8,128)(2,1)S(1)}, bf16[2048,640]{1,0:T(8,128)(2,1)}, u32[]{:S(2)}) copy-start(bf16[2048,640]{1,0:T(8,128)(2,1)} %param.10) | copy-start | bytes 7864324
  7.2 30.0 %all-gather.2.cloned.1.call-start = ((), (), s32[]{:S(2)}) async-start(), calls=%async_computation.2 | async-start | bytes 1802240 | tf_op jit(solution)/shard_map/all_gather | solution.py:14
  16.3 25.4 %copy-start.3 = (f32[2048]{0:T(1024)S(1)}, f32[2048]{0:T(1024)}, u32[]{:S(2)}) copy-start(f32[2048]{0:T(1024)} %param.7) | copy-start | bytes 24580
  16.3 44.1 %reduce-scatter.5.cloned.1.call-start = ((), (), s32[]{:S(2)}) async-start(), calls=%async_computation.4 | async-start | bytes 1351680 | tf_op jit(solution)/shard_map/reduce_scatter | solution.py:23
  41.6 2.9 %copy-start.5 = (f32[2048]{0:T(1024)S(1)}, f32[2048]{0:T(1024)}, u32[]{:S(2)}) copy-start(f32[2048]{0:T(1024)} %param.8) | copy-start | bytes 24580
  41.6 53.4 %reduce-scatter.3.cloned.1.call-start = ((), (), s32[]{:S(2)}) async-start(), calls=%async_computation.3 | async-start | bytes 1351680 | tf_op jit(solution)/shard_map/reduce_scatter | solution.py:24
  41.7 2.8 %copy-start.1 = (bf16[352,2048]{1,0:T(8,128)(2,1)S(1)}, bf16[352,2048]{1,0:T(8,128)(2,1)}, u32[]{:S(2)}) copy-start(bf16[352,2048]{1,0:T(8,128)(2,1)} %all-gather.2.cloned.1.call-done) | copy-start | bytes 4325380
  41.7 2.8 %copy-start.2 = (bf16[2048,640]{1,0:T(8,128)(2,1)S(1)}, bf16[2048,640]{1,0:T(8,128)(2,1)}, u32[]{:S(2)}) copy-start(bf16[2048,640]{1,0:T(8,128)(2,1)} %param.9) | copy-start | bytes 7864324
  46.8 4.5 %copy-start.4 = (s32[352]{0:T(512)S(1)}, s32[352]{0:T(512)}, u32[]{:S(2)}) copy-start(s32[352]{0:T(512)} %param.11) | copy-start | bytes 4228
Sparse Core Ops, SparseCore 0:
  16.4 20.6 all-gather.1
  41.7 18.6 reduce-scatter.4
  62.7 18.6 reduce-scatter.2
where the time goes:
time: 186 us
  blocking collectives  109 us (59%)
  waiting for transfers between devices  29.9 us (16%)
  matrix products  15.7 us (8%)
  between operations  13.9 us (7%)
  local copies, waits for them, and re-layouts  10.4 us (6%)
  other arithmetic  7.09 us (4%)
    pmax x1, blocking collectives, local(): row_top = lax.pmax(jnp.max(logits, axis=1), ('dp', 'vocab'))  33.4 us
    psum x1, blocking collectives, local(): lax.psum(jnp.sum(head_weight.astype(jnp.float32) * product, axis=1), ('dp...  33.1 us
    psum x1, blocking collectives, local(): lax.psum((jnp.sum(scaled_exp, axis=1), jnp.sum(scaled_exp * tangent_logit...  29.7 us
    all_gather x1, waiting for transfers between devices, local(): gathered = lax.all_gather(normed, 'dp', axis=0, tiled=True)  20.8 us
    unnamed x14, local copies, waits for them, and re-layouts  10.4 us
    reduce_scatter x1, waiting for transfers between devices, local(): lax.psum_scatter(logits, 'tensor', scatter_dimension=0, tiled=True)  9.06 us
    all_gather x1, blocking collectives, local(): full_cot = lax.all_gather(cotangent, 'tensor', axis=0, tiled=True)  6.65 us
    dot_general x1, matrix products, local(): lax.dot_general(gathered, full_cot, (((0,), (0,)), ((), ())), preferred_e...  6.26 us
  transfers between devices with their start and end apart: 3, of which 2 were waited for; matrix products, arithmetic and copies ran while one was open for 6% of the time, Pallas kernels for 0%

commit v1 on v0

v1 whole, which is shorter than its diff:
```python
import functools

import jax
import jax.numpy as jnp
from jax import lax
from jax.experimental import pallas as pl
from jax.experimental.pallas import tpu as pltpu
from jax.sharding import PartitionSpec as P

EPSILON = 1e-06
LANES = 128
CHUNKS = 4
MIB = 1024 * 1024


def remote(src, dst, send_sem, recv_sem, device):
    return pltpu.make_async_remote_copy(
        src_ref=src,
        dst_ref=dst,
        send_sem=send_sem,
        recv_sem=recv_sem,
        device_id=device,
        device_id_type=pl.DeviceIdType.MESH,
    )


def merge(parts):
    top = functools.reduce(jnp.maximum, [part[0] for part in parts])
    scales = [jnp.exp(part[0] - top) for part in parts]
    total = sum(part[1] * scale for part, scale in zip(parts, scales))
    weighted = sum(part[2] * scale for part, scale in zip(parts, scales))
    picked = sum(part[3] for part in parts)
    return top, total, weighted, picked


def kernel(
    n_dp, n_v, res_ref, gain_ref, dir_ref, ids_ref, w_hbm, h_hbm, n_out, c_out, g_out,
    x, w, h, normed, hid, tan, lg, tl, tb, rl, rt, eb, co, ss, sl, sz, sp, gz, gp,
    in_sem, out_sem, ss_s, ss_r, xs_s, xs_r, cs_s, cs_r, ls_s, ls_r, ts_s, ts_r, es_s, es_r,
    sl_s, sl_r, sz_s, sz_r, sp_s, sp_r, gz_s, gz_r, gp_s, gp_r,
):
    n_hi = n_dp // 2
    rows, depth = res_ref.shape
    vocab = w.shape[1]
    pad = x.shape[2]
    width = x.shape[3]
    f32, bf16 = jnp.float32, jnp.bfloat16
    me, v, t = lax.axis_index("dp"), lax.axis_index("vocab"), lax.axis_index("tensor")
    core, my_hi = me % 2, me // 2
    other = 1 - t
    place = me * 2 + t
    mate = me + 1 - 2 * core
    core_peer, y_peer = {"dp": mate}, {"tensor": other}
    plane = [(place + k) % (2 * n_dp) for k in range(1, 2 * n_dp)]
    column = [(v + k) % n_v for k in range(1, n_v)]
    ring = [(me + k) % n_dp for k in range(1, n_dp)]

    load_w = pltpu.make_async_copy(w_hbm, w, in_sem.at[0])
    load_h = pltpu.make_async_copy(h_hbm, h, in_sem.at[1])
    load_w.start()
    load_h.start()

    barrier = pltpu.get_barrier_semaphore()
    for p in plane:
        pl.semaphore_signal(
            barrier, inc=1, device_id={"dp": p // 2, "tensor": p % 2},
            device_id_type=pl.DeviceIdType.MESH,
        )
    for z in column:
        pl.semaphore_signal(
            barrier, inc=1, device_id={"vocab": z}, device_id_type=pl.DeviceIdType.MESH
        )

    mask = lax.broadcasted_iota(jnp.int32, (pad, LANES), 0) == lax.broadcasted_iota(
        jnp.int32, (pad, LANES), 1
    )

    def to_row(col):
        return jnp.sum(jnp.where(mask, col, 0.0), axis=0, keepdims=True)

    def to_col(row):
        return jnp.sum(jnp.where(mask, row, 0.0), axis=1, keepdims=True)

    squares = jnp.zeros((pad, 1), f32)
    for c in range(CHUNKS):
        part = res_ref[:, c * width:(c + 1) * width].astype(f32)
        part = jnp.concatenate([part, jnp.zeros((pad - rows, width), f32)], axis=0)
        squares = squares + jnp.sum(part * part, axis=1, keepdims=True)
        x[me, c] = part.astype(bf16)
    ss[me, t] = to_row(squares)

    pl.semaphore_wait(barrier, len(plane) + len(column))

    for p in plane:
        remote(
            ss.at[me, t], ss.at[me, t], ss_s.at[p // 2, p % 2], ss_r.at[me, t],
            {"dp": p // 2, "tensor": p % 2},
        ).start()
    for c in range(CHUNKS):
        remote(x.at[me, c], x.at[me, c], cs_s.at[my_hi, c], cs_r.at[my_hi, c], core_peer).start()
    for c in range(CHUNKS):
        for k in range(1, n_hi):
            hi = (my_hi + k) % n_hi
            remote(
                x.at[me, c], x.at[me, c], xs_s.at[hi, c], xs_r.at[my_hi, c], {"dp": hi * 2 + core}
            ).start()

    def wait_core(hi):
        for c in range(CHUNKS):
            slot = x.at[hi * 2 + 1 - core, c]
            remote(slot, slot, cs_s.at[hi, c], cs_r.at[hi, c], core_peer).wait_recv()

    for p in plane:
        slot = ss.at[p // 2, p % 2]
        remote(
            slot, slot, ss_s.at[p // 2, p % 2], ss_r.at[p // 2, p % 2],
            {"dp": p // 2, "tensor": p % 2},
        ).wait_recv()

    def out_copy(hi):
        return pltpu.make_async_copy(normed.at[hi], n_out.at[hi], out_sem.at[0, hi])

    def send_logits(hi):
        return remote(
            lg.at[hi, other, pl.ds(0, rows)], rl.at[hi], ls_s.at[hi], ls_r.at[hi], y_peer
        )

    def send_tangents(hi):
        return remote(tb.at[hi], rt.at[hi], ts_s.at[hi], ts_r.at[hi], y_peer)

    def pair(hi, first):
        inverse = jnp.concatenate(
            [
                to_col(lax.rsqrt((ss[hi * 2 + k, 0] + ss[hi * 2 + k, 1]) / (2 * depth) + EPSILON))
                for k in range(2)
            ],
            axis=0,
        )
        for c in range(CHUNKS):
            at = slice(c * width, (c + 1) * width)
            block = jnp.concatenate(
                [x[hi * 2, c].astype(f32), x[hi * 2 + 1, c].astype(f32)], axis=0
            )
            unit = (block * inverse).astype(bf16)
            normed[hi, :, at] = unit
            spread = unit.astype(f32)
            hid[:, at] = (spread * gain_ref[:, at]).astype(bf16)
            tan[:, at] = (spread * dir_ref[:, at]).astype(bf16)
        out_copy(hi).start()
        if first:
            load_w.wait()
        logits = jnp.dot(hid[...], w[...], preferred_element_type=f32)
        lg[hi, 0] = logits[:pad]
        lg[hi, 1] = logits[pad:]
        send_logits(hi).start()
        if first:
            load_h.wait()
        tangents = jnp.dot(hid[...], h[...], preferred_element_type=f32) + jnp.dot(
            tan[...], w[...], preferred_element_type=f32
        )
        tl[hi, 0] = tangents[:pad]
        tl[hi, 1] = tangents[pad:]
        tb[hi] = tl[hi, other].astype(bf16)
        send_tangents(hi).start()

    wait_core(my_hi)
    pair(my_hi, True)

    def later(k, carry):
        hi = (my_hi + k) % n_hi
        for c in range(CHUNKS):
            slot = x.at[hi * 2 + core, c]
            remote(slot, slot, xs_s.at[hi, c], xs_r.at[hi, c], {"dp": hi * 2 + core}).wait_recv()
            remote(slot, slot, cs_s.at[hi, c], cs_r.at[hi, c], core_peer).start()
        wait_core(hi)
        pair(hi, False)
        return carry

    lax.fori_loop(1, n_hi, later, 0)

    offset = (me * n_v + v) * vocab
    tokens = ids_ref.shape[1]

    def onehot(block):
        here = lax.broadcasted_iota(jnp.int32, (pad, tokens), 0)
        wanted = lax.broadcasted_iota(jnp.int32, (pad, tokens), 1) == here + block * rows
        ids = jnp.sum(
            jnp.where(wanted & (here < rows), ids_ref[...].astype(f32) + 1.0, 0.0),
            axis=1, keepdims=True,
        ).astype(jnp.int32) - 1
        return lax.broadcasted_iota(jnp.int32, (pad, vocab), 1) == ids - offset

    def send_exp(hi):
        return remote(eb.at[hi, t], eb.at[hi, t], es_s.at[hi], es_r.at[hi], y_peer)

    def finish(k, carry):
        hi = (my_hi + k) % n_hi
        send_logits(hi).wait_recv()
        blank = jnp.zeros((pad - rows, vocab), f32)
        logits = jnp.concatenate([lg[hi, t][:rows] + rl[hi], blank], axis=0)
        send_tangents(hi).wait_recv()
        tangents = tl[hi, t] + rt[hi].astype(f32)
        top = jnp.max(logits, axis=1, keepdims=True)
        scaled = jnp.exp(logits - top)
        eb[hi, t] = scaled.astype(bf16)
        chosen = onehot(hi * 2 + t)
        sl[t, hi, 0:1] = to_row(top)
        sl[t, hi, 1:2] = to_row(jnp.sum(scaled, axis=1, keepdims=True))
        sl[t, hi, 2:3] = to_row(jnp.sum(scaled * tangents, axis=1, keepdims=True))
        sl[t, hi, 3:4] = to_row(jnp.sum(jnp.where(chosen, tangents, 0.0), axis=1, keepdims=True))
        return carry

    lax.fori_loop(0, n_hi, finish, 0)

    sz[v] = sl[t]
    for z in column:
        remote(sz.at[v], sz.at[v], sz_s.at[z], sz_r.at[v], {"vocab": z}).start()
    send_local = remote(sl.at[t], sl.at[t], sl_s.at[0], sl_r.at[0], y_peer)
    send_local.start()
    for hi in range(n_hi):
        send_exp(hi).start()
    for z in column:
        remote(sz.at[z], sz.at[z], sz_s.at[z], sz_r.at[z], {"vocab": z}).wait_recv()
    for hi in range(n_hi):
        joined = merge([[sz[z, hi, i:i + 1] for i in range(4)] for z in range(n_v)])
        for i in range(4):
            sp[me, t, hi, i:i + 1] = joined[i]
    for p in plane:
        remote(
            sp.at[me, t], sp.at[me, t], sp_s.at[p // 2, p % 2], sp_r.at[me, t],
            {"dp": p // 2, "tensor": p % 2},
        ).start()
    for p in plane:
        slot = sp.at[p // 2, p % 2]
        remote(
            slot, slot, sp_s.at[p // 2, p % 2], sp_r.at[p // 2, p % 2],
            {"dp": p // 2, "tensor": p % 2},
        ).wait_recv()
    slot = sl.at[other]
    remote(slot, slot, sl_s.at[0], sl_r.at[0], y_peer).wait_recv()

    def cot_copy(hi):
        return pltpu.make_async_copy(co.at[hi], c_out.at[hi], out_sem.at[1, hi])

    def cotangents(hi, grad):
        slot = eb.at[hi, other]
        remote(slot, slot, es_s.at[hi], es_r.at[hi], y_peer).wait_recv()
        both = []
        for k in range(2):
            top, total, weighted, picked = merge(
                [[sp[d, k, hi, i:i + 1] for i in range(4)] for d in range(n_dp)]
            )
            score = to_col(picked - weighted / total)
            factor = to_col(jnp.exp(sl[k, hi, 0:1] - top) / total)
            probs = eb[hi, k].astype(f32) * factor
            both.append(score * (onehot(hi * 2 + k).astype(f32) - probs))
        co[hi] = jnp.concatenate(both, axis=0).astype(bf16)
        cot_copy(hi).start()
        back = lax.dot_general(
            co[hi], w[...], (((1,), (1,)), ((), ())), preferred_element_type=f32
        )
        return grad + jnp.sum(back * normed[hi].astype(f32), axis=0, keepdims=True)

    gz[v] = lax.fori_loop(0, n_hi, cotangents, jnp.zeros((1, depth), f32))
    for z in column:
        remote(gz.at[v], gz.at[v], gz_s.at[z], gz_r.at[v], {"vocab": z}).start()
    for z in column:
        remote(gz.at[z], gz.at[z], gz_s.at[z], gz_r.at[z], {"vocab": z}).wait_recv()
    gp[me] = sum(gz[z] for z in range(n_v))
    for d in ring:
        remote(gp.at[me], gp.at[me], gp_s.at[d], gp_r.at[me], {"dp": d}).start()
    for d in ring:
        remote(gp.at[d], gp.at[d], gp_s.at[d], gp_r.at[d], {"dp": d}).wait_recv()
    g_out[...] = sum(gp[d] for d in range(n_dp))

    for p in plane:
        device = {"dp": p // 2, "tensor": p % 2}
        mine = ss.at[me, t]
        remote(mine, mine, ss_s.at[p // 2, p % 2], ss_r.at[me, t], device).wait_send()
        mine = sp.at[me, t]
        remote(mine, mine, sp_s.at[p // 2, p % 2], sp_r.at[me, t], device).wait_send()
    for z in column:
        remote(sz.at[v], sz.at[v], sz_s.at[z], sz_r.at[v], {"vocab": z}).wait_send()
        remote(gz.at[v], gz.at[v], gz_s.at[z], gz_r.at[v], {"vocab": z}).wait_send()
    for d in ring:
        remote(gp.at[me], gp.at[me], gp_s.at[d], gp_r.at[me], {"dp": d}).wait_send()
    send_local.wait_send()
    for k in range(n_hi):
        hi = (my_hi + k) % n_hi
        for c in range(CHUNKS):
            mine = x.at[hi * 2 + core, c]
            remote(mine, mine, cs_s.at[hi, c], cs_r.at[hi, c], core_peer).wait_send()
            if k:
                mine = x.at[me, c]
                remote(
                    mine, mine, xs_s.at[hi, c], xs_r.at[my_hi, c], {"dp": hi * 2 + core}
                ).wait_send()
        send_logits(hi).wait_send()
        send_tangents(hi).wait_send()
        send_exp(hi).wait_send()
        out_copy(hi).wait()
        cot_copy(hi).wait()


def local(n_dp, n_v, residual, norm_gain, gain_dir, head_weight, head_dir, sampled):
    n_hi = n_dp // 2
    rows, depth = residual.shape
    vocab = head_weight.shape[1]
    pad = -(-rows // 16) * 16
    f32, bf16 = jnp.float32, jnp.bfloat16
    vmem = pl.BlockSpec(memory_space=pltpu.VMEM)
    hbm = pl.BlockSpec(memory_space=pl.ANY)
    dma = pltpu.SemaphoreType.DMA
    pairs = [
        dma((n_dp, 2)), dma((n_dp, 2)),
        dma((n_hi, CHUNKS)), dma((n_hi, CHUNKS)), dma((n_hi, CHUNKS)), dma((n_hi, CHUNKS)),
        dma((n_hi,)), dma((n_hi,)), dma((n_hi,)), dma((n_hi,)), dma((n_hi,)), dma((n_hi,)),
        dma((1,)), dma((1,)), dma((n_v,)), dma((n_v,)), dma((n_dp, 2)), dma((n_dp, 2)),
        dma((n_v,)), dma((n_v,)), dma((n_dp,)), dma((n_dp,)),
    ]
    normed, cotangent, gain = pl.pallas_call(
        functools.partial(kernel, n_dp, n_v),
        out_shape=(
            jax.ShapeDtypeStruct((n_hi, 2 * pad, depth), bf16),
            jax.ShapeDtypeStruct((n_hi, 2 * pad, vocab), bf16),
            jax.ShapeDtypeStruct((1, depth), f32),
        ),
        in_specs=[vmem, vmem, vmem, vmem, hbm, hbm],
        out_specs=(hbm, hbm, vmem),
        scratch_shapes=[
            pltpu.VMEM((n_dp, CHUNKS, pad, depth // CHUNKS), bf16),
            pltpu.VMEM((depth, vocab), bf16),
            pltpu.VMEM((depth, vocab), bf16),
            pltpu.VMEM((n_hi, 2 * pad, depth), bf16),
            pltpu.VMEM((2 * pad, depth), bf16),
            pltpu.VMEM((2 * pad, depth), bf16),
            pltpu.VMEM((n_hi, 2, pad, vocab), f32),
            pltpu.VMEM((n_hi, 2, pad, vocab), f32),
            pltpu.VMEM((n_hi, pad, vocab), bf16),
            pltpu.VMEM((n_hi, rows, vocab), f32),
            pltpu.VMEM((n_hi, pad, vocab), bf16),
            pltpu.VMEM((n_hi, 2, pad, vocab), bf16),
            pltpu.VMEM((n_hi, 2 * pad, vocab), bf16),
            pltpu.VMEM((n_dp, 2, 1, LANES), f32),
            pltpu.VMEM((2, n_hi, 4, LANES), f32),
            pltpu.VMEM((n_v, n_hi, 4, LANES), f32),
            pltpu.VMEM((n_dp, 2, n_hi, 4, LANES), f32),
            pltpu.VMEM((n_v, 1, depth), f32),
            pltpu.VMEM((n_dp, 1, depth), f32),
            dma((2,)), dma((2, n_hi)),
        ] + pairs,
        compiler_params=pltpu.CompilerParams(
            collective_id=0, has_side_effects=True, vmem_limit_bytes=56 * MIB
        ),
        cost_estimate=pl.CostEstimate(
            flops=8 * n_dp * rows * depth * vocab,
            bytes_accessed=4 * depth * vocab,
            transcendentals=n_dp * rows * vocab,
        ),
    )(
        residual, norm_gain.reshape(1, depth), gain_dir.reshape(1, depth),
        sampled.reshape(1, -1), head_weight, head_dir,
    )
    product = lax.dot_general(
        normed.reshape(n_dp * pad, depth), cotangent.reshape(n_dp * pad, vocab),
        (((0,), (0,)), ((), ())), preferred_element_type=f32,
    )
    return norm_gain[:, None] * product, gain.reshape(depth)


def solution(mesh):
    assert mesh.shape["tensor"] == 2 and mesh.shape["dp"] % 2 == 0
    in_specs = (
        P("dp", "tensor"),
        P("tensor"),
        P("tensor"),
        P("tensor", ("dp", "vocab")),
        P("tensor", ("dp", "vocab")),
        P(),
    )
    out_specs = (P("tensor", ("dp", "vocab")), P("tensor"))
    return jax.shard_map(
        functools.partial(local, mesh.shape["dp"], mesh.shape["vocab"]),
        mesh=mesh, in_specs=in_specs, out_specs=out_specs, check_vma=False,
    )
```

time: 186 us -> 54.7 us (0.29)
  blocking collectives: 109 us -> 0 us
  Pallas kernels: 0 us -> 46.4 us
  waiting for transfers between devices: 29.9 us -> 0 us
  between operations: 13.9 us -> 0.66 us
  matrix products: 15.7 us -> 5.59 us
  local copies, waits for them, and re-layouts: 10.4 us -> 1.85 us
  other arithmetic: 7.09 us -> 0 us
    psum x3 -> x0, blocking collectives: 68.7 us -> none  [the longest x1 33.1 us: local(): lax.psum(jnp.sum(head_weight.astype(jnp.float32) * product, axis=1), ('dp...]
    pallas_call x0 -> x1, Pallas kernels: none -> 46.4 us  [local(): pl.pallas_call(functools.partial(kernel, n_dp, n_v), out_shape=(jax.Shape...]
    pmax x1 -> x0, blocking collectives: 33.4 us -> none  [local(): row_top = lax.pmax(jnp.max(logits, axis=1), ('dp', 'vocab'))]
    all_gather x1 -> x0, waiting for transfers between devices: 20.8 us -> none  [local(): gathered = lax.all_gather(normed, 'dp', axis=0, tiled=True)]
    dot_general x4 -> x1, matrix products: 15.7 us -> 5.59 us  [local(): lax.dot_general(normed.reshape(n_dp * pad, depth), cotangent.reshape(n_dp...]
    unnamed x14 -> x5, local copies, waits for them, and re-layouts: 10.4 us -> 0.61 us
    reduce_scatter x2 -> x0, waiting for transfers between devices: 9.06 us -> none  [the longest x1 9.06 us: local(): lax.psum_scatter(logits, 'tensor', scatter_dimension=0, tiled=True)]
    all_gather x1 -> x0, blocking collectives: 6.65 us -> none  [local(): full_cot = lax.all_gather(cotangent, 'tensor', axis=0, tiled=True)]
  transfers between devices with their start and end apart: 3 -> 0, of which waited for: 2 -> 0; matrix products, arithmetic and copies ran while one was open for 6% -> 0% of each run, Pallas kernels for 0% -> 0%
where the time goes in v1:
time: 54.7 us; the launch traced here: 54.5 us
  Pallas kernels  46.4 us (85%)
  matrix products  5.59 us (10%)
  local copies, waits for them, and re-layouts  1.85 us (3%)
  between operations  0.66 us (1%)
    pallas_call x1, Pallas kernels, local(): pl.pallas_call(functools.partial(kernel, n_dp, n_v), out_shape=(jax.Shape...  46.4 us
    dot_general x1, matrix products, local(): lax.dot_general(normed.reshape(n_dp * pad, depth), cotangent.reshape(n_dp...  5.59 us
    reshape x1, local copies, waits for them, and re-layouts, local(): sampled.reshape(1, -1)  1.25 us

profile of v1, /device:TPU:0, one launch (start us, length us, event | category | flops | bytes accessed | tf_op | source)
XLA Modules:
  0.0 54.5 jit_solution(13036661597208874662)
XLA Ops:
  0.6 1.2 %reshape.21.ids_ref = s32[1,352]{1,0:T(1,128)} reshape(s32[352]{0:T(512)} %param.11) | data formatting | bytes 2816 | tf_op jit(solution)/shard_map/reshape | solution.py:362
  1.9 0.0 copy-start.1
  1.9 46.4 %shard_map.77 = (bf16[2,192,2048]{2,1,0:T(8,128)(2,1)}, bf16[2,192,640]{2,1,0:T(8,128)(2,1)}, f32[1,2048]{1,0:T(1,128)}) custom-call(bf16[88,2048]{1,0:T(8,128)(2,1)} %res_ref.1, f32[1,2048]{1,0:T(1,128)} %bitcast.9, f32[1,2048]{1,0:T(1,128)} %bitcast.8, s32[1,352]{1,0:T(1,128)} %reshape.21.ids_ref, bf16[2048,640]{1,0:T(8,128)(2,1)} %w_hbm.1, ...), custom_call_target="tpu_custom_call" | custom-call | flops 3690987520 | bytes 5242880 | tf_op jit(solution)/shard_map/pallas_call | solution.py:321
  48.3 0.0 copy-done.1
  48.3 0.0 copy-start
  48.3 5.6 %bitcast_multiply_fusion = f32[2048,640]{1,0:T(8,128)} fusion(bf16[2,192,2048]{2,1,0:T(8,128)(2,1)} %get-tuple-element.5, bf16[2,192,640]{2,1,0:T(8,128)(2,1)} %get-tuple-element.6, f32[2048]{0:T(1024)S(1)} %copy-done.1), kind=kOutput, calls=%fused_computation | convolution fusion | flops 1007943680 | bytes 7315456 | tf_op jit(solution)/shard_map/dot_general | solution.py:364
  53.9 0.0 copy-done
  53.9 0.6 %copy.9 = f32[2048]{0:T(1024)} copy(f32[2048]{0:T(1024)S(1)} %bitcast.7) | data formatting | bytes 16384
Async XLA Ops:
  1.9 46.4 %copy-start.1 = (f32[2048]{0:T(1024)S(1)}, f32[2048]{0:T(1024)}, u32[]{:S(2)}) copy-start(f32[2048]{0:T(1024)} %param.7) | copy-start | bytes 24580
  48.3 5.6 %copy-start = (f32[1,2048]{1,0:T(1,128)S(1)}, f32[1,2048]{1,0:T(1,128)}, u32[]{:S(2)}) copy-start(f32[1,2048]{1,0:T(1,128)} %get-tuple-element.7) | copy-start | bytes 24580

commit v2 on v1

v2 whole, which is shorter than its diff:
```python
import functools

import jax
import jax.numpy as jnp
from jax import lax
from jax.experimental import pallas as pl
from jax.experimental.pallas import tpu as pltpu
from jax.sharding import PartitionSpec as P

EPSILON = 1e-06
LANES = 128
CHUNKS = 4
MIB = 1024 * 1024


def remote(src, dst, send_sem, recv_sem, device):
    return pltpu.make_async_remote_copy(
        src_ref=src,
        dst_ref=dst,
        send_sem=send_sem,
        recv_sem=recv_sem,
        device_id=device,
        device_id_type=pl.DeviceIdType.MESH,
    )


def merge(parts):
    top = functools.reduce(jnp.maximum, [part[0] for part in parts])
    scales = [jnp.exp(part[0] - top) for part in parts]
    total = sum(part[1] * scale for part, scale in zip(parts, scales))
    weighted = sum(part[2] * scale for part, scale in zip(parts, scales))
    picked = sum(part[3] for part in parts)
    return top, total, weighted, picked


def kernel(
    n_dp, n_v, res_ref, gain_ref, dir_ref, ids_ref, w_hbm, h_hbm, n_out, c_out, g_out,
    x, w, h, normed, turned, hid, tan, lg, tl, rl, eb, hot, co, na, nb, ss, ml, st, sz, sp, sc,
    gz, gp,
    in_sem, out_sem, ss_s, ss_r, xs_s, xs_r, cs_s, cs_r, ls_s, ls_r, es_s, es_r, ms_s, ms_r,
    sz_s, sz_r, sp_s, sp_r, gz_s, gz_r, gp_s, gp_r,
):
    n_hi = n_dp // 2
    rows, depth = res_ref.shape
    vocab = w.shape[1]
    pad = x.shape[2]
    width = x.shape[3]
    f32, bf16 = jnp.float32, jnp.bfloat16
    me, v, t = lax.axis_index("dp"), lax.axis_index("vocab"), lax.axis_index("tensor")
    core, my_hi = me % 2, me // 2
    other = 1 - t
    place = me * 2 + t
    mate = me + 1 - 2 * core
    core_peer, y_peer = {"dp": mate}, {"tensor": other}
    plane = [(place + k) % (2 * n_dp) for k in range(1, 2 * n_dp)]
    column = [(v + k) % n_v for k in range(1, n_v)]
    ring = [(me + k) % n_dp for k in range(1, n_dp)]

    barrier = pltpu.get_barrier_semaphore()
    for p in plane:
        pl.semaphore_signal(
            barrier, inc=1, device_id={"dp": p // 2, "tensor": p % 2},
            device_id_type=pl.DeviceIdType.MESH,
        )
    for z in column:
        pl.semaphore_signal(
            barrier, inc=1, device_id={"vocab": z}, device_id_type=pl.DeviceIdType.MESH
        )

    load_w = pltpu.make_async_copy(w_hbm, w, in_sem.at[0])
    load_h = pltpu.make_async_copy(h_hbm, h, in_sem.at[1])
    load_w.start()
    load_h.start()

    mask = lax.broadcasted_iota(jnp.int32, (pad, LANES), 0) == lax.broadcasted_iota(
        jnp.int32, (pad, LANES), 1
    )

    def to_row(col):
        return jnp.sum(jnp.where(mask, col, 0.0), axis=0, keepdims=True)

    def to_col(row):
        return jnp.sum(jnp.where(mask, row, 0.0), axis=1, keepdims=True)

    squares = jnp.zeros((pad, 1), f32)
    for c in range(CHUNKS):
        part = res_ref[:, c * width:(c + 1) * width].astype(f32)
        part = jnp.concatenate([part, jnp.zeros((pad - rows, width), f32)], axis=0)
        squares = squares + jnp.sum(part * part, axis=1, keepdims=True)
        x[me, c] = part.astype(bf16)
    ss[me, t] = to_row(squares)

    pl.semaphore_wait(barrier, len(plane) + len(column))

    for p in plane:
        remote(
            ss.at[me, t], ss.at[me, t], ss_s.at[p // 2, p % 2], ss_r.at[me, t],
            {"dp": p // 2, "tensor": p % 2},
        ).start()
    for c in range(CHUNKS):
        remote(x.at[me, c], x.at[me, c], cs_s.at[my_hi, c], cs_r.at[my_hi, c], core_peer).start()
    for c in range(CHUNKS):
        for k in range(1, n_hi):
            hi = (my_hi + k) % n_hi
            remote(
                x.at[me, c], x.at[me, c], xs_s.at[hi, c], xs_r.at[my_hi, c], {"dp": hi * 2 + core}
            ).start()

    def pass_on(hi, c):
        slot = x.at[hi * 2 + core, c]
        remote(slot, slot, xs_s.at[hi, c], xs_r.at[hi, c], {"dp": hi * 2 + core}).wait_recv()
        remote(slot, slot, cs_s.at[hi, c], cs_r.at[hi, c], core_peer).start()

    def wait_core(hi):
        for c in range(CHUNKS):
            slot = x.at[hi * 2 + 1 - core, c]
            remote(slot, slot, cs_s.at[hi, c], cs_r.at[hi, c], core_peer).wait_recv()

    for p in plane:
        slot = ss.at[p // 2, p % 2]
        remote(
            slot, slot, ss_s.at[p // 2, p % 2], ss_r.at[p // 2, p % 2],
            {"dp": p // 2, "tensor": p % 2},
        ).wait_recv()

    def out_copy(hi):
        return pltpu.make_async_copy(turned, n_out.at[hi], out_sem.at[0, hi])

    def cot_copy(hi):
        return pltpu.make_async_copy(co.at[hi], c_out.at[hi], out_sem.at[1, hi])

    def send_logits(hi):
        return remote(
            lg.at[hi, other, pl.ds(0, rows)], rl.at[hi], ls_s.at[hi], ls_r.at[hi], y_peer
        )

    def send_exp(hi):
        return remote(eb.at[hi, t], eb.at[hi, t], es_s.at[hi], es_r.at[hi], y_peer)

    def send_top(hi):
        return remote(ml.at[hi, t], ml.at[hi, t], ms_s.at[hi], ms_r.at[hi], y_peer)

    offset = (me * n_v + v) * vocab
    tokens = ids_ref.shape[0]

    def onehot(block):
        here = lax.broadcasted_iota(jnp.int32, (pad, tokens), 0)
        wanted = lax.broadcasted_iota(jnp.int32, (pad, tokens), 1) == here + block * rows
        ids = jnp.sum(
            jnp.where(wanted & (here < rows), ids_ref[...].reshape(1, tokens).astype(f32) + 1.0, 0.0),
            axis=1, keepdims=True,
        ).astype(jnp.int32) - 1
        return (lax.broadcasted_iota(jnp.int32, (pad, vocab), 1) == ids - offset).astype(f32)

    def pair(hi, first):
        inverse = jnp.concatenate(
            [
                to_col(lax.rsqrt((ss[hi * 2 + k, 0] + ss[hi * 2 + k, 1]) / (2 * depth) + EPSILON))
                for k in range(2)
            ],
            axis=0,
        )
        for c in range(CHUNKS):
            at = slice(c * width, (c + 1) * width)
            block = jnp.concatenate(
                [x[hi * 2, c].astype(f32), x[hi * 2 + 1, c].astype(f32)], axis=0
            )
            unit = (block * inverse).astype(bf16)
            normed[hi, :, at] = unit
            spread = unit.astype(f32)
            hid[:, at] = (spread * gain_ref[:, at]).astype(bf16)
            tan[:, at] = (spread * dir_ref[:, at]).astype(bf16)
        if first:
            load_w.wait()
        logits = jnp.dot(hid[...], w[...], preferred_element_type=f32)
        lg[hi, 0] = logits[:pad]
        lg[hi, 1] = logits[pad:]
        send_logits(hi).start()
        if first:
            load_h.wait()
        tangents = jnp.dot(hid[...], h[...], preferred_element_type=f32) + jnp.dot(
            tan[...], w[...], preferred_element_type=f32
        )
        tl[hi, 0] = tangents[:pad]
        tl[hi, 1] = tangents[pad:]
        hot[hi] = jnp.concatenate([onehot(hi * 2), onehot(hi * 2 + 1)], axis=0).astype(bf16)
        if not first:
            out_copy((hi + n_hi - 1) % n_hi).wait()
        turned[...] = normed[hi].T
        out_copy(hi).start()

    def finish(hi):
        send_logits(hi).wait_recv()
        blank = jnp.zeros((pad - rows, vocab), f32)
        logits = jnp.concatenate([lg[hi, t][:rows] + rl[hi], blank], axis=0)
        top = jnp.max(logits, axis=1, keepdims=True)
        eb[hi, t] = jnp.exp(logits - top).astype(bf16)
        ml[hi, t] = to_row(top)
        send_exp(hi).start()
        send_top(hi).start()

    def sums(hi, k):
        block = hi * 2 + k
        scaled, tangents = eb[hi, k].astype(f32), tl[hi, k]
        chosen = hot[hi, pl.ds(pl.multiple_of(k * pad, 16), pad)].astype(f32)
        at = pl.ds(block, 1)
        st[0, at] = ml[hi, k]
        st[1, at] = to_row(jnp.sum(scaled, axis=1, keepdims=True))
        st[2, at] = to_row(jnp.sum(scaled * tangents, axis=1, keepdims=True))
        st[3, at] = to_row(jnp.sum(chosen * tangents, axis=1, keepdims=True))

    def wait_exp(hi):
        slot = eb.at[hi, other]
        remote(slot, slot, es_s.at[hi], es_r.at[hi], y_peer).wait_recv()
        slot = ml.at[hi, other]
        remote(slot, slot, ms_s.at[hi], ms_r.at[hi], y_peer).wait_recv()

    def back(hi, k, carry=None):
        at = pl.ds(pl.multiple_of(k * pad, 16), pad)
        unit = normed[hi, at].astype(f32)
        turn = (((1,), (1,)), ((), ()))
        na[hi, k] = unit * lax.dot_general(hot[hi, at], w[...], turn, preferred_element_type=f32)
        nb[hi, k] = unit * lax.dot_general(eb[hi, k], w[...], turn, preferred_element_type=f32)

    wait_core(my_hi)
    pair(my_hi, True)

    def later(k, carry):
        hi = (my_hi + k) % n_hi
        for c in range(CHUNKS - 1):
            pass_on(hi, c)
        finish((my_hi + k - 1) % n_hi)
        pass_on(hi, CHUNKS - 1)
        wait_core(hi)
        pair(hi, False)
        return carry

    def early(k, carry):
        hi = (my_hi + k) % n_hi
        sums(hi, t)
        wait_exp(hi)
        sums(hi, other)
        return carry

    lax.fori_loop(1, n_hi, later, 0)
    last = (my_hi + n_hi - 1) % n_hi
    lax.fori_loop(0, n_hi - 1, early, 0)
    finish(last)
    sums(last, t)
    back(my_hi, t)
    wait_exp(last)
    sums(last, other)

    sz[v] = st[...]
    for z in column:
        remote(sz.at[v], sz.at[v], sz_s.at[z], sz_r.at[v], {"vocab": z}).start()
    back(my_hi, other)
    for z in column:
        remote(sz.at[z], sz.at[z], sz_s.at[z], sz_r.at[z], {"vocab": z}).wait_recv()
    joined = merge([[sz[z, i] for i in range(4)] for z in range(n_v)])
    for i in range(4):
        sp[me, t, i] = joined[i]
    for p in plane:
        remote(
            sp.at[me, t], sp.at[me, t], sp_s.at[p // 2, p % 2], sp_r.at[me, t],
            {"dp": p // 2, "tensor": p % 2},
        ).start()

    def rest(k, carry):
        hi = (my_hi + k) % n_hi
        back(hi, 0)
        back(hi, 1)
        return carry

    lax.fori_loop(1, n_hi, rest, 0)
    for p in plane:
        slot = sp.at[p // 2, p % 2]
        remote(
            slot, slot, sp_s.at[p // 2, p % 2], sp_r.at[p // 2, p % 2],
            {"dp": p // 2, "tensor": p % 2},
        ).wait_recv()
    top, total, weighted, picked = merge(
        [[sp[d, k, i] for i in range(4)] for d in range(n_dp) for k in range(2)]
    )
    total = 0.5 * total
    sc[0] = picked - weighted / total
    sc[1] = jnp.exp(st[0] - top) / total

    def gain_part(hi, grad):
        for k in range(2):
            at = pl.ds(hi * 2 + k, 1)
            score, factor = to_col(sc[0, at]), to_col(sc[1, at])
            grad = grad + jnp.sum(
                score * (na[hi, k] - factor * nb[hi, k]), axis=0, keepdims=True
            )
        return grad

    gz[v] = lax.fori_loop(0, n_hi, gain_part, jnp.zeros((1, depth), f32))
    for z in column:
        remote(gz.at[v], gz.at[v], gz_s.at[z], gz_r.at[v], {"vocab": z}).start()

    def cotangents(hi, carry):
        both = []
        for k in range(2):
            at = pl.ds(hi * 2 + k, 1)
            score, factor = to_col(sc[0, at]), to_col(sc[1, at])
            chosen = hot[hi, k * pad:(k + 1) * pad].astype(f32)
            both.append(score * (chosen - eb[hi, k].astype(f32) * factor))
        co[hi] = jnp.concatenate(both, axis=0).astype(bf16)
        cot_copy(hi).start()
        return carry

    lax.fori_loop(0, n_hi, cotangents, 0)
    for z in column:
        remote(gz.at[z], gz.at[z], gz_s.at[z], gz_r.at[z], {"vocab": z}).wait_recv()
    gp[me] = sum(gz[z] for z in range(n_v))
    for d in ring:
        remote(gp.at[me], gp.at[me], gp_s.at[d], gp_r.at[me], {"dp": d}).start()
    for d in ring:
        remote(gp.at[d], gp.at[d], gp_s.at[d], gp_r.at[d], {"dp": d}).wait_recv()
    g_out[...] = sum(gp[d] for d in range(n_dp))

    for p in plane:
        device = {"dp": p // 2, "tensor": p % 2}
        mine = ss.at[me, t]
        remote(mine, mine, ss_s.at[p // 2, p % 2], ss_r.at[me, t], device).wait_send()
        mine = sp.at[me, t]
        remote(mine, mine, sp_s.at[p // 2, p % 2], sp_r.at[me, t], device).wait_send()
    for z in column:
        remote(sz.at[v], sz.at[v], sz_s.at[z], sz_r.at[v], {"vocab": z}).wait_send()
        remote(gz.at[v], gz.at[v], gz_s.at[z], gz_r.at[v], {"vocab": z}).wait_send()
    for d in ring:
        remote(gp.at[me], gp.at[me], gp_s.at[d], gp_r.at[me], {"dp": d}).wait_send()
    for k in range(n_hi):
        hi = (my_hi + k) % n_hi
        for c in range(CHUNKS):
            mine = x.at[hi * 2 + core, c]
            remote(mine, mine, cs_s.at[hi, c], cs_r.at[hi, c], core_peer).wait_send()
            if k:
                mine = x.at[me, c]
                remote(
                    mine, mine, xs_s.at[hi, c], xs_r.at[my_hi, c], {"dp": hi * 2 + core}
                ).wait_send()
        send_logits(hi).wait_send()
        send_exp(hi).wait_send()
        send_top(hi).wait_send()
        cot_copy(hi).wait()
    out_copy(last).wait()


def last_kernel(turned, cot, gain_ref, sum_ref, head_ref, sum_out):
    tile = head_ref.shape[0]
    mask = lax.broadcasted_iota(jnp.int32, (tile, tile), 0) == lax.broadcasted_iota(
        jnp.int32, (tile, tile), 1
    )
    gain = jnp.sum(jnp.where(mask, gain_ref[...], 0.0), axis=1, keepdims=True)
    product = sum(
        jnp.dot(turned[hi], cot[hi], preferred_element_type=jnp.float32)
        for hi in range(turned.shape[0])
    )
    head_ref[...] = gain * product
    sum_out[...] = sum_ref[...]


def local(n_dp, n_v, residual, norm_gain, gain_dir, head_weight, head_dir, sampled):
    n_hi = n_dp // 2
    rows, depth = residual.shape
    vocab = head_weight.shape[1]
    pad = -(-rows // 16) * 16
    f32, bf16 = jnp.float32, jnp.bfloat16
    vmem = pl.BlockSpec(memory_space=pltpu.VMEM)
    hbm = pl.BlockSpec(memory_space=pl.ANY)
    dma = pltpu.SemaphoreType.DMA
    pairs = [
        dma((n_dp, 2)), dma((n_dp, 2)),
        dma((n_hi, CHUNKS)), dma((n_hi, CHUNKS)), dma((n_hi, CHUNKS)), dma((n_hi, CHUNKS)),
        dma((n_hi,)), dma((n_hi,)), dma((n_hi,)), dma((n_hi,)), dma((n_hi,)), dma((n_hi,)),
        dma((n_v,)), dma((n_v,)), dma((n_dp, 2)), dma((n_dp, 2)),
        dma((n_v,)), dma((n_v,)), dma((n_dp,)), dma((n_dp,)),
    ]
    gain_row = norm_gain.reshape(1, depth)
    turned, cotangent, gain = pl.pallas_call(
        functools.partial(kernel, n_dp, n_v),
        out_shape=(
            jax.ShapeDtypeStruct((n_hi, depth, 2 * pad), bf16),
            jax.ShapeDtypeStruct((n_hi, 2 * pad, vocab), bf16),
            jax.ShapeDtypeStruct((1, depth), f32),
        ),
        in_specs=[vmem, vmem, vmem, vmem, hbm, hbm],
        out_specs=(hbm, hbm, vmem),
        scratch_shapes=[
            pltpu.VMEM((n_dp, CHUNKS, pad, depth // CHUNKS), bf16),
            pltpu.VMEM((depth, vocab), bf16),
            pltpu.VMEM((depth, vocab), bf16),
            pltpu.VMEM((n_hi, 2 * pad, depth), bf16),
            pltpu.VMEM((depth, 2 * pad), bf16),
            pltpu.VMEM((2 * pad, depth), bf16),
            pltpu.VMEM((2 * pad, depth), bf16),
            pltpu.VMEM((n_hi, 2, pad, vocab), f32),
            pltpu.VMEM((n_hi, 2, pad, vocab), f32),
            pltpu.VMEM((n_hi, rows, vocab), f32),
            pltpu.VMEM((n_hi, 2, pad, vocab), bf16),
            pltpu.VMEM((n_hi, 2 * pad, vocab), bf16),
            pltpu.VMEM((n_hi, 2 * pad, vocab), bf16),
            pltpu.VMEM((n_hi, 2, pad, depth), f32),
            pltpu.VMEM((n_hi, 2, pad, depth), f32),
            pltpu.VMEM((n_dp, 2, 1, LANES), f32),
            pltpu.VMEM((n_hi, 2, 1, LANES), f32),
            pltpu.VMEM((4, n_dp, LANES), f32),
            pltpu.VMEM((n_v, 4, n_dp, LANES), f32),
            pltpu.VMEM((n_dp, 2, 4, n_dp, LANES), f32),
            pltpu.VMEM((2, n_dp, LANES), f32),
            pltpu.VMEM((n_v, 1, depth), f32),
            pltpu.VMEM((n_dp, 1, depth), f32),
            dma((2,)), dma((2, n_hi)),
        ] + pairs,
        compiler_params=pltpu.CompilerParams(
            collective_id=0, has_side_effects=True, vmem_limit_bytes=62 * MIB
        ),
        cost_estimate=pl.CostEstimate(
            flops=10 * n_dp * rows * depth * vocab,
            bytes_accessed=4 * depth * vocab,
            transcendentals=n_dp * rows * vocab,
        ),
    )(residual, gain_row, gain_dir.reshape(1, depth), sampled, head_weight, head_dir)
    tile = depth // 8
    fisher_head, fisher_gain = pl.pallas_call(
        last_kernel,
        grid=(depth // tile,),
        out_shape=(
            jax.ShapeDtypeStruct((depth, vocab), f32),
            jax.ShapeDtypeStruct((1, depth), f32),
        ),
        in_specs=[
            pl.BlockSpec((n_hi, tile, 2 * pad), lambda i: (0, i, 0)),
            pl.BlockSpec((n_hi, 2 * pad, vocab), lambda i: (0, 0, 0)),
            pl.BlockSpec((1, tile), lambda i: (0, i)),
            pl.BlockSpec((1, tile), lambda i: (0, i)),
        ],
        out_specs=(
            pl.BlockSpec((tile, vocab), lambda i: (i, 0)),
            pl.BlockSpec((1, tile), lambda i: (0, i)),
        ),
        compiler_params=pltpu.CompilerParams(vmem_limit_bytes=62 * MIB),
        cost_estimate=pl.CostEstimate(
            flops=2 * n_dp * rows * depth * vocab,
            bytes_accessed=4 * depth * vocab,
            transcendentals=0,
        ),
    )(turned, cotangent, gain_row, gain)
    return fisher_head, fisher_gain.reshape(depth)


def solution(mesh):
    assert mesh.shape["tensor"] == 2 and mesh.shape["dp"] % 2 == 0
    in_specs = (
        P("dp", "tensor"),
        P("tensor"),
        P("tensor"),
        P("tensor", ("dp", "vocab")),
        P("tensor", ("dp", "vocab")),
        P(),
    )
    out_specs = (P("tensor", ("dp", "vocab")), P("tensor"))
    return jax.shard_map(
        functools.partial(local, mesh.shape["dp"], mesh.shape["vocab"]),
        mesh=mesh, in_specs=in_specs, out_specs=out_specs, check_vma=False,
    )
```

time: 54.7 us -> 55.4 us (1.013)
  Pallas kernels: 46.4 us -> 54.5 us
  matrix products: 5.59 us -> 0 us
  local copies, waits for them, and re-layouts: 1.85 us -> 0 us
    pallas_call x0 -> x1, Pallas kernels: none -> 7.66 us  [local(): pl.pallas_call(last_kernel, grid=(depth // tile,), out_shape=(jax.ShapeDt...]
    dot_general x1 -> x0, matrix products: 5.59 us -> none  [local(): lax.dot_general(normed.reshape(n_dp * pad, depth), cotangent.reshape(n_dp...]
    reshape x1 -> x0, local copies, waits for them, and re-layouts: 1.25 us -> none  [local(): sampled.reshape(1, -1)]
    unnamed x5 -> x0, local copies, waits for them, and re-layouts: 0.61 us -> none
where the time goes in v2:
time: 55.4 us; the launch traced here: 55.1 us
  Pallas kernels  54.5 us (98%)
  between operations  0.64 us (1%)
    pallas_call x1, Pallas kernels, local(): pl.pallas_call(functools.partial(kernel, n_dp, n_v), out_shape=(jax.Shape...  46.8 us
    pallas_call x1, Pallas kernels, local(): pl.pallas_call(last_kernel, grid=(depth // tile,), out_shape=(jax.ShapeDt...  7.66 us

profile of v2, /device:TPU:0, one launch (start us, length us, event | category | flops | bytes accessed | tf_op | source)
XLA Modules:
  0.0 55.1 jit_solution(11618775713775656740)
XLA Ops:
  0.6 46.8 %shard_map.77 = (bf16[2,2048,192]{2,1,0:T(8,128)(2,1)}, bf16[2,192,640]{2,1,0:T(8,128)(2,1)}, f32[1,2048]{1,0:T(1,128)}) custom-call(bf16[88,2048]{1,0:T(8,128)(2,1)} %res_ref.1, f32[1,2048]{1,0:T(1,128)} %bitcast.4, f32[1,2048]{1,0:T(1,128)} %bitcast.3, s32[352]{0:T(512)} %ids_ref.1, bf16[2048,640]{1,0:T(8,128)(2,1)} %w_hbm.1, bf16[2048,640]{1,0:T(8,128)(2,1)} %h_hbm.1), custom_call_target="tpu_custom_call" | custom-call | flops 4613734400 | bytes 5242880 | tf_op jit(solution)/shard_map/pallas_call | solution.py:382
  47.4 7.7 %shard_map.78 = (f32[2048,640]{1,0:T(8,128)}, f32[1,2048]{1,0:T(1,128)}) custom-call(bf16[2,2048,192]{2,1,0:T(8,128)(2,1)} %get-tuple-element.7.turned, bf16[2,192,640]{2,1,0:T(8,128)(2,1)} %get-tuple-element.8.cot, f32[1,2048]{1,0:T(1,128)} %bitcast.5, f32[1,2048]{1,0:T(1,128)} %get-tuple-element.9.sum_ref), custom_call_target="tpu_custom_call" | custom-call | flops 922746880 | bytes 5242880 | tf_op jit(solution)/shard_map/pallas_call | solution.py:427

commit v3 on v2

v3 whole, which is shorter than its diff:
```python
import functools

import jax
import jax.numpy as jnp
from jax import lax
from jax.experimental import pallas as pl
from jax.experimental.pallas import tpu as pltpu
from jax.sharding import PartitionSpec as P

EPSILON = 1e-06
LANES = 128
CHUNKS = 4
MIB = 1024 * 1024


def remote(src, dst, send_sem, recv_sem, device):
    return pltpu.make_async_remote_copy(
        src_ref=src,
        dst_ref=dst,
        send_sem=send_sem,
        recv_sem=recv_sem,
        device_id=device,
        device_id_type=pl.DeviceIdType.MESH,
    )


def merge(parts):
    top = functools.reduce(jnp.maximum, [part[0] for part in parts])
    scales = [jnp.exp(part[0] - top) for part in parts]
    total = sum(part[1] * scale for part, scale in zip(parts, scales))
    weighted = sum(part[2] * scale for part, scale in zip(parts, scales))
    picked = sum(part[3] for part in parts)
    return top, total, weighted, picked


def kernel(
    n_dp, n_v, res_ref, gain_ref, dir_ref, ids_ref, w_hbm, h_hbm, head_out, g_out,
    x, w, h, normed, hid, tan, lg, tl, rl, he, na, nb, stage, ss, ml, st, sz, sp, sc,
    gz, gp,
    in_sem, out_sem, ss_s, ss_r, xs_s, xs_r, zs_s, zs_r, cs_s, cs_r, ls_s, ls_r, es_s, es_r, ms_s, ms_r,
    sz_s, sz_r, sp_s, sp_r, gz_s, gz_r, gp_s, gp_r,
):
    n_hi = n_dp // 2
    rows, depth = res_ref.shape
    vocab = w.shape[1]
    pad = x.shape[2]
    width = x.shape[3]
    f32, bf16 = jnp.float32, jnp.bfloat16
    me, v, t = lax.axis_index("dp"), lax.axis_index("vocab"), lax.axis_index("tensor")
    core, my_hi = me % 2, me // 2
    other = 1 - t
    place = me * 2 + t
    mate = me + 1 - 2 * core
    core_peer, y_peer = {"dp": mate}, {"tensor": other}
    side = v % 2
    z_peer = {"vocab": v + 1 - 2 * side}
    half = CHUNKS // 2
    plane = [(place + k) % (2 * n_dp) for k in range(1, 2 * n_dp)]
    column = [(v + k) % n_v for k in range(1, n_v)]
    ring = [(me + k) % n_dp for k in range(1, n_dp)]

    barrier = pltpu.get_barrier_semaphore()
    for p in plane:
        pl.semaphore_signal(
            barrier, inc=1, device_id={"dp": p // 2, "tensor": p % 2},
            device_id_type=pl.DeviceIdType.MESH,
        )
    for z in column:
        pl.semaphore_signal(
            barrier, inc=1, device_id={"vocab": z}, device_id_type=pl.DeviceIdType.MESH
        )

    load_w = pltpu.make_async_copy(w_hbm, w, in_sem.at[0])
    load_h = pltpu.make_async_copy(h_hbm, h, in_sem.at[1])
    load_w.start()
    load_h.start()

    mask = lax.broadcasted_iota(jnp.int32, (pad, LANES), 0) == lax.broadcasted_iota(
        jnp.int32, (pad, LANES), 1
    )

    def to_row(col):
        return jnp.sum(jnp.where(mask, col, 0.0), axis=0, keepdims=True)

    def to_col(row):
        return jnp.sum(jnp.where(mask, row, 0.0), axis=1, keepdims=True)

    squares = jnp.zeros((pad, 1), f32)
    for c in range(CHUNKS):
        part = res_ref[:, c * width:(c + 1) * width].astype(f32)
        part = jnp.concatenate([part, jnp.zeros((pad - rows, width), f32)], axis=0)
        squares = squares + jnp.sum(part * part, axis=1, keepdims=True)
        x[me, c] = part.astype(bf16)
    ss[me, t] = to_row(squares)

    offset = (me * n_v + v) * vocab
    tokens = ids_ref.shape[0]

    def onehot(block):
        here = lax.broadcasted_iota(jnp.int32, (pad, tokens), 0)
        wanted = lax.broadcasted_iota(jnp.int32, (pad, tokens), 1) == here + block * rows
        ids = jnp.sum(
            jnp.where(wanted & (here < rows), ids_ref[...].reshape(1, tokens).astype(f32) + 1.0, 0.0),
            axis=1, keepdims=True,
        ).astype(jnp.int32) - 1
        return (lax.broadcasted_iota(jnp.int32, (pad, vocab), 1) == ids - offset).astype(
            f32
        ).astype(bf16)

    def mark(hi, carry):
        for k in range(2):
            he[hi, k] = onehot(hi * 2 + k)
        return carry

    pl.semaphore_wait(barrier, len(plane) + len(column))

    for p in plane:
        remote(
            ss.at[me, t], ss.at[me, t], ss_s.at[p // 2, p % 2], ss_r.at[me, t],
            {"dp": p // 2, "tensor": p % 2},
        ).start()
    for c in range(CHUNKS):
        remote(x.at[me, c], x.at[me, c], cs_s.at[my_hi, c], cs_r.at[my_hi, c], core_peer).start()
    def send_block(hi, j):
        c = side * half + j
        return remote(
            x.at[me, c], x.at[me, c], xs_s.at[hi, j], xs_r.at[my_hi, j], {"dp": hi * 2 + core}
        )

    def send_side(hi, j):
        slot = x.at[hi * 2 + core, side * half + j]
        return remote(slot, slot, zs_s.at[hi, j], zs_r.at[hi, j], z_peer)

    def send_core(hi, c):
        slot = x.at[hi * 2 + core, c]
        return remote(slot, slot, cs_s.at[hi, c], cs_r.at[hi, c], core_peer)

    for j in range(half):
        for k in range(1, n_hi):
            send_block((my_hi + k) % n_hi, j).start()

    def pass_on(hi, j):
        c = side * half + j
        slot = x.at[hi * 2 + core, c]
        remote(slot, slot, xs_s.at[hi, j], xs_r.at[hi, j], {"dp": hi * 2 + core}).wait_recv()
        send_side(hi, j).start()
        send_core(hi, c).start()

    def pass_side(hi, j):
        c = (1 - side) * half + j
        slot = x.at[hi * 2 + core, c]
        remote(slot, slot, zs_s.at[hi, j], zs_r.at[hi, j], z_peer).wait_recv()
        send_core(hi, c).start()

    def wait_core(hi):
        for c in range(CHUNKS):
            slot = x.at[hi * 2 + 1 - core, c]
            remote(slot, slot, cs_s.at[hi, c], cs_r.at[hi, c], core_peer).wait_recv()

    lax.fori_loop(0, n_hi, mark, 0)
    for p in plane:
        slot = ss.at[p // 2, p % 2]
        remote(
            slot, slot, ss_s.at[p // 2, p % 2], ss_r.at[p // 2, p % 2],
            {"dp": p // 2, "tensor": p % 2},
        ).wait_recv()

    def send_logits(hi):
        return remote(
            lg.at[hi, other, pl.ds(0, rows)], rl.at[hi], ls_s.at[hi], ls_r.at[hi], y_peer
        )

    def send_exp(hi):
        return remote(he.at[hi, 2 + t], he.at[hi, 2 + t], es_s.at[hi], es_r.at[hi], y_peer)

    def send_top(hi):
        return remote(ml.at[hi, t], ml.at[hi, t], ms_s.at[hi], ms_r.at[hi], y_peer)

    def pair(hi, first):
        inverse = jnp.concatenate(
            [
                to_col(lax.rsqrt((ss[hi * 2 + k, 0] + ss[hi * 2 + k, 1]) / (2 * depth) + EPSILON))
                for k in range(2)
            ],
            axis=0,
        )
        for c in range(CHUNKS):
            at = slice(c * width, (c + 1) * width)
            block = jnp.concatenate(
                [x[hi * 2, c].astype(f32), x[hi * 2 + 1, c].astype(f32)], axis=0
            )
            unit = (block * inverse).astype(bf16)
            normed[hi, :, at] = unit
            spread = unit.astype(f32)
            hid[:, at] = (spread * gain_ref[:, at]).astype(bf16)
            tan[:, at] = (spread * dir_ref[:, at]).astype(bf16)
        if first:
            load_w.wait()
        logits = jnp.dot(hid[...], w[...], preferred_element_type=f32)
        lg[hi, 0] = logits[:pad]
        lg[hi, 1] = logits[pad:]
        send_logits(hi).start()
        if first:
            load_h.wait()
        tangents = jnp.dot(hid[...], h[...], preferred_element_type=f32) + jnp.dot(
            tan[...], w[...], preferred_element_type=f32
        )
        tl[hi, 0] = tangents[:pad]
        tl[hi, 1] = tangents[pad:]

    def finish(hi):
        send_logits(hi).wait_recv()
        blank = jnp.zeros((pad - rows, vocab), f32)
        logits = jnp.concatenate([lg[hi, t][:rows] + rl[hi], blank], axis=0)
        top = jnp.max(logits, axis=1, keepdims=True)
        he[hi, 2 + t] = jnp.exp(logits - top).astype(bf16)
        ml[hi, t] = to_row(top)
        send_exp(hi).start()
        send_top(hi).start()

    def sums(hi, k):
        block = hi * 2 + k
        scaled, tangents = he[hi, 2 + k].astype(f32), tl[hi, k]
        chosen = he[hi, k].astype(f32)
        at = pl.ds(block, 1)
        st[0, at] = ml[hi, k]
        st[1, at] = to_row(jnp.sum(scaled, axis=1, keepdims=True))
        st[2, at] = to_row(jnp.sum(scaled * tangents, axis=1, keepdims=True))
        st[3, at] = to_row(jnp.sum(chosen * tangents, axis=1, keepdims=True))

    def wait_exp(hi):
        slot = he.at[hi, 2 + other]
        remote(slot, slot, es_s.at[hi], es_r.at[hi], y_peer).wait_recv()
        slot = ml.at[hi, other]
        remote(slot, slot, ms_s.at[hi], ms_r.at[hi], y_peer).wait_recv()

    def back(hi, part):
        at = slice(part * depth // 2, (part + 1) * depth // 2)
        both = jnp.concatenate([he[hi, k].astype(f32) for k in range(4)], axis=0).astype(bf16)
        turned = lax.dot_general(
            both, w[at], (((1,), (1,)), ((), ())), preferred_element_type=f32
        )
        unit = normed[hi, :, at].astype(f32)
        na[hi, :, at] = unit * turned[:2 * pad]
        nb[hi, :, at] = unit * turned[2 * pad:]

    wait_core(my_hi)
    pair(my_hi, True)

    def later(k, carry):
        hi = (my_hi + k) % n_hi
        for j in range(half):
            pass_on(hi, j)
        for j in range(half - 1):
            pass_side(hi, j)
        finish((my_hi + k - 1) % n_hi)
        pass_side(hi, half - 1)
        wait_core(hi)
        pair(hi, False)
        return carry

    def early(k, carry):
        hi = (my_hi + k) % n_hi
        sums(hi, t)
        wait_exp(hi)
        sums(hi, other)
        back(hi, 0)
        back(hi, 1)
        return carry

    lax.fori_loop(1, n_hi, later, 0)
    last = (my_hi + n_hi - 1) % n_hi
    lax.fori_loop(0, n_hi - 1, early, 0)
    finish(last)
    sums(last, t)
    wait_exp(last)
    sums(last, other)

    sz[v] = st[...]
    for z in column:
        remote(sz.at[v], sz.at[v], sz_s.at[z], sz_r.at[v], {"vocab": z}).start()
    back(last, 0)
    for z in column:
        remote(sz.at[z], sz.at[z], sz_s.at[z], sz_r.at[z], {"vocab": z}).wait_recv()
    joined = merge([[sz[z, i] for i in range(4)] for z in range(n_v)])
    for i in range(4):
        sp[me, t, i] = joined[i]
    for p in plane:
        remote(
            sp.at[me, t], sp.at[me, t], sp_s.at[p // 2, p % 2], sp_r.at[me, t],
            {"dp": p // 2, "tensor": p % 2},
        ).start()

    back(last, 1)
    for p in plane:
        slot = sp.at[p // 2, p % 2]
        remote(
            slot, slot, sp_s.at[p // 2, p % 2], sp_r.at[p // 2, p % 2],
            {"dp": p // 2, "tensor": p % 2},
        ).wait_recv()
    top, total, weighted, picked = merge(
        [[sp[d, k, i] for i in range(4)] for d in range(n_dp) for k in range(2)]
    )
    total = 0.5 * total
    sc[0] = picked - weighted / total
    sc[1] = jnp.exp(st[0] - top) / total

    def gain_part(hi, grad):
        for k in range(2):
            at, here = pl.ds(hi * 2 + k, 1), slice(k * pad, (k + 1) * pad)
            score, factor = to_col(sc[0, at]), to_col(sc[1, at])
            grad = grad + jnp.sum(
                score * (na[hi, here] - factor * nb[hi, here]), axis=0, keepdims=True
            )
        return grad

    gz[v] = lax.fori_loop(0, n_hi, gain_part, jnp.zeros((1, depth), f32))
    for z in column:
        remote(gz.at[v], gz.at[v], gz_s.at[z], gz_r.at[v], {"vocab": z}).start()

    def cotangents(hi, carry):
        for k in range(2):
            at = pl.ds(hi * 2 + k, 1)
            score, factor = to_col(sc[0, at]), to_col(sc[1, at])
            chosen = he[hi, k].astype(f32)
            he[hi, k] = (score * (chosen - he[hi, 2 + k].astype(f32) * factor)).astype(bf16)
        return carry

    lax.fori_loop(0, n_hi, cotangents, 0)

    slots, tile = stage.shape[0], stage.shape[1]
    tiles = depth // tile
    square = lax.broadcasted_iota(jnp.int32, (tile, tile), 0) == lax.broadcasted_iota(
        jnp.int32, (tile, tile), 1
    )

    def head_copy(i):
        return pltpu.make_async_copy(
            stage.at[i % slots], head_out.at[pl.ds(i * tile, tile)], out_sem.at[i % slots]
        )

    def head_tile(i):
        at = slice(i * tile, (i + 1) * tile)
        product = sum(
            lax.dot_general(
                normed[hi, :, at], he[hi, 0:2].reshape(2 * pad, vocab), (((0,), (0,)), ((), ())),
                preferred_element_type=f32,
            )
            for hi in range(n_hi)
        )
        if i >= slots:
            head_copy(i - slots).wait()
        gain = jnp.sum(jnp.where(square, gain_ref[:, at], 0.0), axis=1, keepdims=True)
        stage[i % slots] = gain * product
        head_copy(i).start()

    for i in range(tiles // 2):
        head_tile(i)
    for z in column:
        remote(gz.at[z], gz.at[z], gz_s.at[z], gz_r.at[z], {"vocab": z}).wait_recv()
    gp[me] = sum(gz[z] for z in range(n_v))
    for d in ring:
        remote(gp.at[me], gp.at[me], gp_s.at[d], gp_r.at[me], {"dp": d}).start()
    for i in range(tiles // 2, tiles):
        head_tile(i)
    for d in ring:
        remote(gp.at[d], gp.at[d], gp_s.at[d], gp_r.at[d], {"dp": d}).wait_recv()
    g_out[...] = sum(gp[d] for d in range(n_dp))

    for p in plane:
        device = {"dp": p // 2, "tensor": p % 2}
        mine = ss.at[me, t]
        remote(mine, mine, ss_s.at[p // 2, p % 2], ss_r.at[me, t], device).wait_send()
        mine = sp.at[me, t]
        remote(mine, mine, sp_s.at[p // 2, p % 2], sp_r.at[me, t], device).wait_send()
    for z in column:
        remote(sz.at[v], sz.at[v], sz_s.at[z], sz_r.at[v], {"vocab": z}).wait_send()
        remote(gz.at[v], gz.at[v], gz_s.at[z], gz_r.at[v], {"vocab": z}).wait_send()
    for d in ring:
        remote(gp.at[me], gp.at[me], gp_s.at[d], gp_r.at[me], {"dp": d}).wait_send()
    for k in range(n_hi):
        hi = (my_hi + k) % n_hi
        for c in range(CHUNKS):
            send_core(hi, c).wait_send()
        if k:
            for j in range(half):
                send_block(hi, j).wait_send()
                send_side(hi, j).wait_send()
        send_logits(hi).wait_send()
        send_exp(hi).wait_send()
        send_top(hi).wait_send()
    for i in range(max(tiles - slots, 0), tiles):
        head_copy(i).wait()


def local(n_dp, n_v, residual, norm_gain, gain_dir, head_weight, head_dir, sampled):
    n_hi = n_dp // 2
    rows, depth = residual.shape
    vocab = head_weight.shape[1]
    pad = -(-rows // 16) * 16
    f32, bf16 = jnp.float32, jnp.bfloat16
    vmem = pl.BlockSpec(memory_space=pltpu.VMEM)
    hbm = pl.BlockSpec(memory_space=pl.ANY)
    dma = pltpu.SemaphoreType.DMA
    pairs = [
        dma((n_dp, 2)), dma((n_dp, 2)),
        dma((n_hi, CHUNKS)), dma((n_hi, CHUNKS)), dma((n_hi, CHUNKS)), dma((n_hi, CHUNKS)),
        dma((n_hi, CHUNKS)), dma((n_hi, CHUNKS)),
        dma((n_hi,)), dma((n_hi,)), dma((n_hi,)), dma((n_hi,)), dma((n_hi,)), dma((n_hi,)),
        dma((n_v,)), dma((n_v,)), dma((n_dp, 2)), dma((n_dp, 2)),
        dma((n_v,)), dma((n_v,)), dma((n_dp,)), dma((n_dp,)),
    ]
    tile = depth // 8
    slots = 4 if n_dp <= 4 else 2
    fisher_head, fisher_gain = pl.pallas_call(
        functools.partial(kernel, n_dp, n_v),
        out_shape=(
            jax.ShapeDtypeStruct((depth, vocab), f32),
            jax.ShapeDtypeStruct((1, depth), f32),
        ),
        in_specs=[vmem, vmem, vmem, vmem] + [hbm, hbm],
        out_specs=(hbm, vmem),
        scratch_shapes=[
            pltpu.VMEM((n_dp, CHUNKS, pad, depth // CHUNKS), bf16),
            pltpu.VMEM((depth, vocab), bf16),
            pltpu.VMEM((depth, vocab), bf16),
            pltpu.VMEM((n_hi, 2 * pad, depth), bf16),
            pltpu.VMEM((2 * pad, depth), bf16),
            pltpu.VMEM((2 * pad, depth), bf16),
            pltpu.VMEM((n_hi, 2, pad, vocab), f32),
            pltpu.VMEM((n_hi, 2, pad, vocab), f32),
            pltpu.VMEM((n_hi, rows, vocab), f32),
            pltpu.VMEM((n_hi, 4, pad, vocab), bf16),
            pltpu.VMEM((n_hi, 2 * pad, depth), f32),
            pltpu.VMEM((n_hi, 2 * pad, depth), f32),
            pltpu.VMEM((slots, tile, vocab), f32),
            pltpu.VMEM((n_dp, 2, 1, LANES), f32),
            pltpu.VMEM((n_hi, 2, 1, LANES), f32),
            pltpu.VMEM((4, n_dp, LANES), f32),
            pltpu.VMEM((n_v, 4, n_dp, LANES), f32),
            pltpu.VMEM((n_dp, 2, 4, n_dp, LANES), f32),
            pltpu.VMEM((2, n_dp, LANES), f32),
            pltpu.VMEM((n_v, 1, depth), f32),
            pltpu.VMEM((n_dp, 1, depth), f32),
            dma((2,)), dma((slots,)),
        ] + pairs,
        compiler_params=pltpu.CompilerParams(
            collective_id=0, has_side_effects=True, vmem_limit_bytes=(36 if n_dp <= 4 else 62) * MIB
        ),
        cost_estimate=pl.CostEstimate(
            flops=10 * n_dp * rows * depth * vocab,
            bytes_accessed=4 * depth * vocab,
            transcendentals=n_dp * rows * vocab,
        ),
    )(residual, norm_gain.reshape(1, depth), gain_dir.reshape(1, depth), sampled, head_weight, head_dir)
    return fisher_head, fisher_gain.reshape(depth)


def solution(mesh):
    assert mesh.shape["tensor"] == 2 and mesh.shape["dp"] % 2 == 0
    in_specs = (
        P("dp", "tensor"),
        P("tensor"),
        P("tensor"),
        P("tensor", ("dp", "vocab")),
        P("tensor", ("dp", "vocab")),
        P(),
    )
    out_specs = (P("tensor", ("dp", "vocab")), P("tensor"))
    return jax.shard_map(
        functools.partial(local, mesh.shape["dp"], mesh.shape["vocab"]),
        mesh=mesh, in_specs=in_specs, out_specs=out_specs, check_vma=False,
    )
```

time: 55.4 us -> 56.6 us (1.022)
  local copies, waits for them, and re-layouts: 0 us -> 9.49 us
  Pallas kernels: 54.5 us -> 46.2 us
    unnamed x0 -> x14, local copies, waits for them, and re-layouts: none -> 9.49 us
    pallas_call x1 -> x0, Pallas kernels: 7.66 us -> none  [local(): pl.pallas_call(last_kernel, grid=(depth // tile,), out_shape=(jax.ShapeDt...]
    pallas_call x1, Pallas kernels: 46.8 us -> 46.2 us  [local(): pl.pallas_call(functools.partial(kernel, n_dp, n_v), out_shape=(jax.Shape...]
where the time goes in v3:
time: 56.6 us; the launch traced here: 56.3 us
  Pallas kernels  46.2 us (82%)
  local copies, waits for them, and re-layouts  9.49 us (17%)
  between operations  0.65 us (1%)
    pallas_call x1, Pallas kernels, local(): pl.pallas_call(functools.partial(kernel, n_dp, n_v), out_shape=(jax.Shape...  46.2 us
    unnamed x14, local copies, waits for them, and re-layouts  9.49 us

profile of v3, /device:TPU:0, one launch (start us, length us, event | category | flops | bytes accessed | tf_op | source)
XLA Modules:
  0.0 56.3 jit_solution(13578226070067034960)
XLA Ops:
  0.6 0.0 copy-start
  0.6 1.7 %copy-done = bf16[2048,640]{1,0:T(8,128)(2,1)S(1)} copy-done((bf16[2048,640]{1,0:T(8,128)(2,1)S(1)}, bf16[2048,640]{1,0:T(8,128)(2,1)}, u32[]{:S(2)}) %copy-start) | copy-done | bytes 2621464
  2.4 0.0 copy-start.1
  2.4 1.7 %copy-done.1 = bf16[2048,640]{1,0:T(8,128)(2,1)S(1)} copy-done((bf16[2048,640]{1,0:T(8,128)(2,1)S(1)}, bf16[2048,640]{1,0:T(8,128)(2,1)}, u32[]{:S(2)}) %copy-start.1) | copy-done | bytes 2621464
  4.1 0.0 copy-start.2
  4.1 1.0 %copy-done.2 = bf16[88,2048]{1,0:T(8,128)(2,1)S(1)} copy-done((bf16[88,2048]{1,0:T(8,128)(2,1)S(1)}, bf16[88,2048]{1,0:T(8,128)(2,1)}, u32[]{:S(2)}) %copy-start.2) | copy-done | bytes 360472
  5.1 0.0 copy-start.3
  5.1 0.7 %copy-done.3 = f32[2048]{0:T(1024)S(1)} copy-done((f32[2048]{0:T(1024)S(1)}, f32[2048]{0:T(1024)}, u32[]{:S(2)}) %copy-start.3) | copy-done | bytes 8216
  5.8 0.0 copy-start.4
  5.8 0.7 %copy-done.4 = f32[2048]{0:T(1024)S(1)} copy-done((f32[2048]{0:T(1024)S(1)}, f32[2048]{0:T(1024)}, u32[]{:S(2)}) %copy-start.4) | copy-done | bytes 8216
  6.5 0.0 copy-start.5
  6.5 0.7 %copy-done.5 = s32[352]{0:T(512)S(1)} copy-done((s32[352]{0:T(512)S(1)}, s32[352]{0:T(512)}, u32[]{:S(2)}) %copy-start.5) | copy-done | bytes 1432
  7.2 46.2 %shard_map.77 = (f32[2048,640]{1,0:T(8,128)S(1)}, f32[1,2048]{1,0:T(1,128)S(1)}) custom-call(bf16[88,2048]{1,0:T(8,128)(2,1)S(1)} %copy-done.2, f32[1,2048]{1,0:T(1,128)S(1)} %bitcast.4, f32[1,2048]{1,0:T(1,128)S(1)} %bitcast.5, s32[352]{0:T(512)S(1)} %copy-done.5, bf16[2048,640]{1,0:T(8,128)(2,1)S(1)} %copy-done, bf16[2048,640]{1,0:T(8,128)(2,1)S(1)} %copy-done.1), custom_call_target="tpu_custom_call" | custom-call | flops 4613734400 | bytes 5242880 | tf_op jit(solution)/shard_map/pallas_call | solution.py:415
  53.3 2.4 %copy.10 = f32[2048,640]{1,0:T(8,128)} copy(f32[2048,640]{1,0:T(8,128)S(1)} %get-tuple-element.8) | data formatting | bytes 10485760
  55.7 0.6 %copy.11 = f32[2048]{0:T(1024)} copy(f32[2048]{0:T(1024)S(1)} %bitcast.3) | data formatting | bytes 16384
Async XLA Ops:
  0.6 1.7 %copy-start = (bf16[2048,640]{1,0:T(8,128)(2,1)S(1)}, bf16[2048,640]{1,0:T(8,128)(2,1)}, u32[]{:S(2)}) copy-start(bf16[2048,640]{1,0:T(8,128)(2,1)} %w_hbm.1) | copy-start | bytes 7864324
  2.4 1.7 %copy-start.1 = (bf16[2048,640]{1,0:T(8,128)(2,1)S(1)}, bf16[2048,640]{1,0:T(8,128)(2,1)}, u32[]{:S(2)}) copy-start(bf16[2048,640]{1,0:T(8,128)(2,1)} %h_hbm.1) | copy-start | bytes 7864324
  4.1 1.0 %copy-start.2 = (bf16[88,2048]{1,0:T(8,128)(2,1)S(1)}, bf16[88,2048]{1,0:T(8,128)(2,1)}, u32[]{:S(2)}) copy-start(bf16[88,2048]{1,0:T(8,128)(2,1)} %res_ref.1) | copy-start | bytes 1081348
  5.1 0.7 %copy-start.3 = (f32[2048]{0:T(1024)S(1)}, f32[2048]{0:T(1024)}, u32[]{:S(2)}) copy-start(f32[2048]{0:T(1024)} %param.7) | copy-start | bytes 24580
  5.8 0.7 %copy-start.4 = (f32[2048]{0:T(1024)S(1)}, f32[2048]{0:T(1024)}, u32[]{:S(2)}) copy-start(f32[2048]{0:T(1024)} %param.8) | copy-start | bytes 24580
  6.5 0.7 %copy-start.5 = (s32[352]{0:T(512)S(1)}, s32[352]{0:T(512)}, u32[]{:S(2)}) copy-start(s32[352]{0:T(512)} %ids_ref.1) | copy-start | bytes 4228

commit v4 on v3

--- a/solution.py
+++ b/solution.py
@@ -251,12 +251,11 @@
         hi = (my_hi + k) % n_hi
         for j in range(half):
             pass_on(hi, j)
-        for j in range(half - 1):
+        for j in range(half):
             pass_side(hi, j)
-        finish((my_hi + k - 1) % n_hi)
-        pass_side(hi, half - 1)
         wait_core(hi)
         pair(hi, False)
+        finish((my_hi + k - 1) % n_hi)
         return carry
 
     def early(k, carry):
@@ -445,7 +444,7 @@
             dma((2,)), dma((slots,)),
         ] + pairs,
         compiler_params=pltpu.CompilerParams(
-            collective_id=0, has_side_effects=True, vmem_limit_bytes=(36 if n_dp <= 4 else 62) * MIB
+            collective_id=0, has_side_effects=True, vmem_limit_bytes=62 * MIB
         ),
         cost_estimate=pl.CostEstimate(
             flops=10 * n_dp * rows * depth * vocab,

time: 56.6 us -> 57.6 us (1.018)
  Pallas kernels: 46.2 us -> 51 us
  local copies, waits for them, and re-layouts: 9.49 us -> 5.79 us
    pallas_call x1, Pallas kernels: 46.2 us -> 51 us  [local(): pl.pallas_call(functools.partial(kernel, n_dp, n_v), out_shape=(jax.Shape...]
    unnamed x14 -> x4, local copies, waits for them, and re-layouts: 9.49 us -> 5.79 us
where the time goes in v4:
time: 57.6 us; the launch traced here: 57.4 us
  Pallas kernels  51 us (89%)
  local copies, waits for them, and re-layouts  5.79 us (10%)
  between operations  0.65 us (1%)
    pallas_call x1, Pallas kernels, local(): pl.pallas_call(functools.partial(kernel, n_dp, n_v), out_shape=(jax.Shape...  51 us
    unnamed x4, local copies, waits for them, and re-layouts  5.79 us

profile of v4, /device:TPU:0, one launch (start us, length us, event | category | flops | bytes accessed | tf_op | source)
XLA Modules:
  0.0 57.4 jit_solution(13142610997061534958)
XLA Ops:
  0.6 51.0 %shard_map.77 = (f32[2048,640]{1,0:T(8,128)}, f32[1,2048]{1,0:T(1,128)}) custom-call(bf16[88,2048]{1,0:T(8,128)(2,1)} %res_ref.1, f32[1,2048]{1,0:T(1,128)} %bitcast.4, f32[1,2048]{1,0:T(1,128)} %bitcast.5, s32[352]{0:T(512)} %ids_ref.1, bf16[2048,640]{1,0:T(8,128)(2,1)} %w_hbm.1, bf16[2048,640]{1,0:T(8,128)(2,1)} %h_hbm.1), custom_call_target="tpu_custom_call" | custom-call | flops 4613734400 | bytes 5242880 | tf_op jit(solution)/shard_map/pallas_call | solution.py:414
  51.6 0.0 copy-start
  51.7 5.2 %copy.10 = f32[2048,640]{1,0:T(8,128)} copy(f32[2048,640]{1,0:T(8,128)} %get-tuple-element.8) | data formatting | bytes 10485760
  56.8 0.0 copy-done
  56.8 0.6 %copy.11 = f32[2048]{0:T(1024)} copy(f32[2048]{0:T(1024)S(1)} %bitcast.3) | data formatting | bytes 16384
Async XLA Ops:
  51.6 5.2 %copy-start = (f32[1,2048]{1,0:T(1,128)S(1)}, f32[1,2048]{1,0:T(1,128)}, u32[]{:S(2)}) copy-start(f32[1,2048]{1,0:T(1,128)} %get-tuple-element.5) | copy-start | bytes 24580

commit v5 on v3

--- a/solution.py
+++ b/solution.py
@@ -34,8 +34,8 @@
 
 
 def kernel(
-    n_dp, n_v, res_ref, gain_ref, dir_ref, ids_ref, w_hbm, h_hbm, head_out, g_out,
-    x, w, h, normed, hid, tan, lg, tl, rl, he, na, nb, stage, ss, ml, st, sz, sp, sc,
+    n_dp, n_v, res_ref, gain_ref, dir_ref, ids_ref, w_hbm, h_hbm, n_out, c_out, g_out,
+    x, w, h, normed, hid, tan, lg, tl, rl, he, na, nb, ss, ml, st, sz, sp, sc,
     gz, gp,
     in_sem, out_sem, ss_s, ss_r, xs_s, xs_r, zs_s, zs_r, cs_s, cs_r, ls_s, ls_r, es_s, es_r, ms_s, ms_r,
     sz_s, sz_r, sp_s, sp_r, gz_s, gz_r, gp_s, gp_r,
@@ -165,6 +165,12 @@
             {"dp": p // 2, "tensor": p % 2},
         ).wait_recv()
 
+    def out_copy(hi):
+        return pltpu.make_async_copy(normed.at[hi], n_out.at[hi], out_sem.at[0, hi])
+
+    def cot_copy(hi):
+        return pltpu.make_async_copy(he.at[hi, pl.ds(0, 2)], c_out.at[hi], out_sem.at[1, hi])
+
     def send_logits(hi):
         return remote(
             lg.at[hi, other, pl.ds(0, rows)], rl.at[hi], ls_s.at[hi], ls_r.at[hi], y_peer
@@ -194,6 +200,7 @@
             spread = unit.astype(f32)
             hid[:, at] = (spread * gain_ref[:, at]).astype(bf16)
             tan[:, at] = (spread * dir_ref[:, at]).astype(bf16)
+        out_copy(hi).start()
         if first:
             load_w.wait()
         logits = jnp.dot(hid[...], w[...], preferred_element_type=f32)
@@ -324,45 +331,15 @@
             score, factor = to_col(sc[0, at]), to_col(sc[1, at])
             chosen = he[hi, k].astype(f32)
             he[hi, k] = (score * (chosen - he[hi, 2 + k].astype(f32) * factor)).astype(bf16)
+        cot_copy(hi).start()
         return carry
 
     lax.fori_loop(0, n_hi, cotangents, 0)
-
-    slots, tile = stage.shape[0], stage.shape[1]
-    tiles = depth // tile
-    square = lax.broadcasted_iota(jnp.int32, (tile, tile), 0) == lax.broadcasted_iota(
-        jnp.int32, (tile, tile), 1
-    )
-
-    def head_copy(i):
-        return pltpu.make_async_copy(
-            stage.at[i % slots], head_out.at[pl.ds(i * tile, tile)], out_sem.at[i % slots]
-        )
-
-    def head_tile(i):
-        at = slice(i * tile, (i + 1) * tile)
-        product = sum(
-            lax.dot_general(
-                normed[hi, :, at], he[hi, 0:2].reshape(2 * pad, vocab), (((0,), (0,)), ((), ())),
-                preferred_element_type=f32,
-            )
-            for hi in range(n_hi)
-        )
-        if i >= slots:
-            head_copy(i - slots).wait()
-        gain = jnp.sum(jnp.where(square, gain_ref[:, at], 0.0), axis=1, keepdims=True)
-        stage[i % slots] = gain * product
-        head_copy(i).start()
-
-    for i in range(tiles // 2):
-        head_tile(i)
     for z in column:
         remote(gz.at[z], gz.at[z], gz_s.at[z], gz_r.at[z], {"vocab": z}).wait_recv()
     gp[me] = sum(gz[z] for z in range(n_v))
     for d in ring:
         remote(gp.at[me], gp.at[me], gp_s.at[d], gp_r.at[me], {"dp": d}).start()
-    for i in range(tiles // 2, tiles):
-        head_tile(i)
     for d in ring:
         remote(gp.at[d], gp.at[d], gp_s.at[d], gp_r.at[d], {"dp": d}).wait_recv()
     g_out[...] = sum(gp[d] for d in range(n_dp))
@@ -389,8 +366,8 @@
         send_logits(hi).wait_send()
         send_exp(hi).wait_send()
         send_top(hi).wait_send()
-    for i in range(max(tiles - slots, 0), tiles):
-        head_copy(i).wait()
+        out_copy(hi).wait()
+        cot_copy(hi).wait()
 
 
 def local(n_dp, n_v, residual, norm_gain, gain_dir, head_weight, head_dir, sampled):
@@ -410,16 +387,15 @@
         dma((n_v,)), dma((n_v,)), dma((n_dp, 2)), dma((n_dp, 2)),
         dma((n_v,)), dma((n_v,)), dma((n_dp,)), dma((n_dp,)),
     ]
-    tile = depth // 8
-    slots = 4 if n_dp <= 4 else 2
-    fisher_head, fisher_gain = pl.pallas_call(
+    normed, cotangent, gain = pl.pallas_call(
         functools.partial(kernel, n_dp, n_v),
         out_shape=(
-            jax.ShapeDtypeStruct((depth, vocab), f32),
+            jax.ShapeDtypeStruct((n_hi, 2 * pad, depth), bf16),
+            jax.ShapeDtypeStruct((n_hi, 2, pad, vocab), bf16),
             jax.ShapeDtypeStruct((1, depth), f32),
         ),
         in_specs=[vmem, vmem, vmem, vmem] + [hbm, hbm],
-        out_specs=(hbm, vmem),
+        out_specs=(hbm, hbm, vmem),
         scratch_shapes=[
             pltpu.VMEM((n_dp, CHUNKS, pad, depth // CHUNKS), bf16),
             pltpu.VMEM((depth, vocab), bf16),
@@ -433,7 +409,6 @@
             pltpu.VMEM((n_hi, 4, pad, vocab), bf16),
             pltpu.VMEM((n_hi, 2 * pad, depth), f32),
             pltpu.VMEM((n_hi, 2 * pad, depth), f32),
-            pltpu.VMEM((slots, tile, vocab), f32),
             pltpu.VMEM((n_dp, 2, 1, LANES), f32),
             pltpu.VMEM((n_hi, 2, 1, LANES), f32),
             pltpu.VMEM((4, n_dp, LANES), f32),
@@ -442,10 +417,10 @@
             pltpu.VMEM((2, n_dp, LANES), f32),
             pltpu.VMEM((n_v, 1, depth), f32),
             pltpu.VMEM((n_dp, 1, depth), f32),
-            dma((2,)), dma((slots,)),
+            dma((2,)), dma((2, n_hi)),
         ] + pairs,
         compiler_params=pltpu.CompilerParams(
-            collective_id=0, has_side_effects=True, vmem_limit_bytes=(36 if n_dp <= 4 else 62) * MIB
+            collective_id=0, has_side_effects=True, vmem_limit_bytes=62 * MIB
         ),
         cost_estimate=pl.CostEstimate(
             flops=10 * n_dp * rows * depth * vocab,
@@ -453,7 +428,11 @@
             transcendentals=n_dp * rows * vocab,
         ),
     )(residual, norm_gain.reshape(1, depth), gain_dir.reshape(1, depth), sampled, head_weight, head_dir)
-    return fisher_head, fisher_gain.reshape(depth)
+    product = lax.dot_general(
+        normed.reshape(n_dp * pad, depth), cotangent.reshape(n_dp * pad, vocab),
+        (((0,), (0,)), ((), ())), preferred_element_type=f32,
+    )
+    return norm_gain[:, None] * product, gain.reshape(depth)
 
 
 def solution(mesh):

time: 56.6 us -> 54 us (0.954)
  local copies, waits for them, and re-layouts: 9.49 us -> 0.61 us
  matrix products: 0 us -> 5.59 us
  Pallas kernels: 46.2 us -> 46.9 us
    unnamed x14 -> x5, local copies, waits for them, and re-layouts: 9.49 us -> 0.61 us
    dot_general x0 -> x1, matrix products: none -> 5.59 us  [local(): lax.dot_general(normed.reshape(n_dp * pad, depth), cotangent.reshape(n_dp...]
    pallas_call x1, Pallas kernels: 46.2 us -> 46.9 us  [local(): pl.pallas_call(functools.partial(kernel, n_dp, n_v), out_shape=(jax.Shape...]
where the time goes in v5:
time: 54 us; the launch traced here: 53.8 us
  Pallas kernels  46.9 us (87%)
  matrix products  5.59 us (10%)
  between operations  0.66 us (1%)
  local copies, waits for them, and re-layouts  0.61 us (1%)
    pallas_call x1, Pallas kernels, local(): pl.pallas_call(functools.partial(kernel, n_dp, n_v), out_shape=(jax.Shape...  46.9 us
    dot_general x1, matrix products, local(): lax.dot_general(normed.reshape(n_dp * pad, depth), cotangent.reshape(n_dp...  5.59 us

profile of v5, /device:TPU:0, one launch (start us, length us, event | category | flops | bytes accessed | tf_op | source)
XLA Modules:
  0.0 53.8 jit_solution(10334297899071409091)
XLA Ops:
  0.6 0.0 copy-start
  0.6 46.9 %shard_map.77 = (bf16[2,192,2048]{2,1,0:T(8,128)(2,1)}, bf16[2,2,96,640]{3,2,1,0:T(8,128)(2,1)}, f32[1,2048]{1,0:T(1,128)}) custom-call(bf16[88,2048]{1,0:T(8,128)(2,1)} %res_ref.1, f32[1,2048]{1,0:T(1,128)} %bitcast.9, f32[1,2048]{1,0:T(1,128)} %bitcast.11, s32[352]{0:T(512)} %ids_ref.1, bf16[2048,640]{1,0:T(8,128)(2,1)} %w_hbm.1, bf16[2048,640]{1,0:T(8,128)(2,1)} %h_hbm.1), custom_call_target="tpu_custom_call" | custom-call | flops 4613734400 | bytes 5242880 | tf_op jit(solution)/shard_map/pallas_call | solution.py:390
  47.6 0.0 copy-done
  47.6 0.0 copy-start.1
  47.6 5.6 %convolution_multiply_fusion = f32[2048,640]{1,0:T(8,128)} fusion(bf16[384,2048]{1,0:T(8,128)(2,1)} %bitcast.7, bf16[384,640]{1,0:T(8,128)(2,1)} %bitcast.8, f32[2048]{0:T(1024)S(1)} %copy-done), kind=kOutput, calls=%fused_computation | convolution fusion | flops 1007943680 | bytes 7315456 | tf_op jit(solution)/shard_map/dot_general | solution.py:431
  53.2 0.0 copy-done.1
  53.2 0.6 %copy.9 = f32[2048]{0:T(1024)} copy(f32[2048]{0:T(1024)S(1)} %bitcast.10) | data formatting | bytes 16384
Async XLA Ops:
  0.6 47.0 %copy-start = (f32[2048]{0:T(1024)S(1)}, f32[2048]{0:T(1024)}, u32[]{:S(2)}) copy-start(f32[2048]{0:T(1024)} %param.7) | copy-start | bytes 24580
  47.6 5.6 %copy-start.1 = (f32[1,2048]{1,0:T(1,128)S(1)}, f32[1,2048]{1,0:T(1,128)}, u32[]{:S(2)}) copy-start(f32[1,2048]{1,0:T(1,128)} %get-tuple-element.7) | copy-start | bytes 24580

commit v6 on v5

--- a/solution.py
+++ b/solution.py
@@ -271,6 +271,10 @@
         sums(hi, t)
         wait_exp(hi)
         sums(hi, other)
+        return carry
+
+    def early_back(k, carry):
+        hi = (my_hi + k) % n_hi
         back(hi, 0)
         back(hi, 1)
         return carry
@@ -280,6 +284,7 @@
     lax.fori_loop(0, n_hi - 1, early, 0)
     finish(last)
     sums(last, t)
+    lax.fori_loop(0, n_hi - 1, early_back, 0)
     wait_exp(last)
     sums(last, other)
 

time: 54 us -> 54 us (level)
  no operation moved by 1% of the time
where the time goes in v6:
time: 54 us; the launch traced here: 53.8 us
  Pallas kernels  46.9 us (87%)
  matrix products  5.59 us (10%)
  between operations  0.66 us (1%)
  local copies, waits for them, and re-layouts  0.61 us (1%)
    pallas_call x1, Pallas kernels, local(): pl.pallas_call(functools.partial(kernel, n_dp, n_v), out_shape=(jax.Shape...  46.9 us
    dot_general x1, matrix products, local(): lax.dot_general(normed.reshape(n_dp * pad, depth), cotangent.reshape(n_dp...  5.59 us

profile of v6, /device:TPU:0, one launch (start us, length us, event | category | flops | bytes accessed | tf_op | source)
XLA Modules:
  0.0 53.8 jit_solution(7520844746265550481)
XLA Ops:
  0.6 0.0 copy-start
  0.6 46.9 %shard_map.77 = (bf16[2,192,2048]{2,1,0:T(8,128)(2,1)}, bf16[2,2,96,640]{3,2,1,0:T(8,128)(2,1)}, f32[1,2048]{1,0:T(1,128)}) custom-call(bf16[88,2048]{1,0:T(8,128)(2,1)} %res_ref.1, f32[1,2048]{1,0:T(1,128)} %bitcast.9, f32[1,2048]{1,0:T(1,128)} %bitcast.11, s32[352]{0:T(512)} %ids_ref.1, bf16[2048,640]{1,0:T(8,128)(2,1)} %w_hbm.1, bf16[2048,640]{1,0:T(8,128)(2,1)} %h_hbm.1), custom_call_target="tpu_custom_call" | custom-call | flops 4613734400 | bytes 5242880 | tf_op jit(solution)/shard_map/pallas_call | solution.py:395
  47.6 0.0 copy-done
  47.6 0.0 copy-start.1
  47.6 5.6 %convolution_multiply_fusion = f32[2048,640]{1,0:T(8,128)} fusion(bf16[384,2048]{1,0:T(8,128)(2,1)} %bitcast.7, bf16[384,640]{1,0:T(8,128)(2,1)} %bitcast.8, f32[2048]{0:T(1024)S(1)} %copy-done), kind=kOutput, calls=%fused_computation | convolution fusion | flops 1007943680 | bytes 7315456 | tf_op jit(solution)/shard_map/dot_general | solution.py:436
  53.2 0.0 copy-done.1
  53.2 0.6 %copy.9 = f32[2048]{0:T(1024)} copy(f32[2048]{0:T(1024)S(1)} %bitcast.10) | data formatting | bytes 16384
Async XLA Ops:
  0.6 47.0 %copy-start = (f32[2048]{0:T(1024)S(1)}, f32[2048]{0:T(1024)}, u32[]{:S(2)}) copy-start(f32[2048]{0:T(1024)} %param.7) | copy-start | bytes 24580
  47.6 5.6 %copy-start.1 = (f32[1,2048]{1,0:T(1,128)S(1)}, f32[1,2048]{1,0:T(1,128)}, u32[]{:S(2)}) copy-start(f32[1,2048]{1,0:T(1,128)} %get-tuple-element.7) | copy-start | bytes 24580
